TPU v7x, 32 devices: a whole 2x2x4 slice. The times are simulated.
32 devices in a mesh: dp: 8 (over z, core), space: 4 (over y, x).
Axes of the slice: x: 2, y: 2, z: 4, core: 2. Of those that a mesh axis runs over, the one named last changes fastest.
Arguments:
- cotangent: bfloat16 [8, 24, 128, 1024], P('dp', None, 'space'), may hold values from -6 to 6
- spectrum: float32 [64, 8, 24, 128], P('space', 'dp'), may hold values from -6 to 6
- weights: float32 [64, 24, 24, 128], P('space'), may hold values from -0.875 to 0.875
Outputs:
- grad_input: bfloat16 [8, 24, 128, 1024], P('dp', None, 'space')
- grad_weights: float32 [64, 576, 128], P('space', 'dp')
All inputs are finite; a program needn't handle non-finite values.
Results may differ from a plain program's by a relative error of at most 0.001.
Values sent between devices are 32-bit elements; how exact they have to be, the bound alone decides.
A program may use at most 64 MiB of HBM per device.

v0:
```python
import math

import jax
import jax.numpy as jnp
from jax import lax
from jax.sharding import PartitionSpec as P


def column_basis(col_count, modes_y):
    position = jnp.arange(col_count, dtype=jnp.int32)
    frequency = jnp.arange(modes_y, dtype=jnp.int32)
    phase = position[:, None] * frequency[None, :] % col_count
    angles = phase.astype(jnp.float32) * (2.0 * math.pi / col_count)
    return jnp.concatenate([jnp.cos(angles), -jnp.sin(angles)], axis=1)


def row_basis(mode_count, first_row, row_count, height):
    frequency = jnp.arange(mode_count, dtype=jnp.int32)
    position = first_row + jnp.arange(row_count, dtype=jnp.int32)
    phase = frequency[:, None] * position[None, :] % height
    angles = phase.astype(jnp.float32) * (2.0 * math.pi / height)
    return (jnp.cos(angles), jnp.sin(angles))


def spectral_backward(spec_grad, weights, modes_y):
    hp = lax.Precision.HIGHEST
    grad_re, grad_im = (spec_grad[..., :modes_y], spec_grad[..., modes_y:])
    weight_re, weight_im = (weights[..., :modes_y], weights[..., modes_y:])
    real_part = jnp.einsum("kbox,kcox->kbcx", grad_re, weight_re, precision=hp) + jnp.einsum(
        "kbox,kcox->kbcx", grad_im, weight_im, precision=hp
    )
    imag_part = jnp.einsum("kbox,kcox->kbcx", grad_im, weight_re, precision=hp) - jnp.einsum(
        "kbox,kcox->kbcx", grad_re, weight_im, precision=hp
    )
    return jnp.concatenate([real_part, imag_part], axis=-1)


def weight_terms(spectrum, spec_grad, modes_y):
    hp = lax.Precision.HIGHEST
    spec_re, spec_im = (spectrum[..., :modes_y], spectrum[..., modes_y:])
    grad_re, grad_im = (spec_grad[..., :modes_y], spec_grad[..., modes_y:])
    real_part = jnp.einsum("kbcx,kbox->kcox", spec_re, grad_re, precision=hp) + jnp.einsum(
        "kbcx,kbox->kcox", spec_im, grad_im, precision=hp
    )
    imag_part = jnp.einsum("kbcx,kbox->kcox", spec_re, grad_im, precision=hp) - jnp.einsum(
        "kbcx,kbox->kcox", spec_im, grad_re, precision=hp
    )
    joined = jnp.concatenate([real_part, imag_part], axis=-1)
    return joined.reshape(joined.shape[0], joined.shape[1] * joined.shape[2], joined.shape[3])


def body(cotangent, spectrum, weights):
    hp = lax.Precision.HIGHEST
    space_count = lax.axis_size("space")
    raster_count, channels, row_count, col_count = cotangent.shape
    local_modes = spectrum.shape[0]
    modes_y = spectrum.shape[3] // 2
    height = row_count * space_count
    basis = column_basis(col_count, modes_y)
    first_row = lax.axis_index("space") * row_count
    col_spec = jnp.einsum(
        "rcxw,wj->rcxj", cotangent, basis, precision=hp, preferred_element_type=jnp.float32
    )
    forward_scale = 1.0 / math.sqrt(height * col_count)
    cosines, sines = row_basis(local_modes * lax.axis_size("space"), first_row, row_count, height)
    with_cos = jnp.einsum("kx,rcxj->krcj", cosines, col_spec, precision=hp)
    with_sin = jnp.einsum("kx,rcxj->krcj", sines, col_spec, precision=hp)
    joined = jnp.concatenate(
        [
            with_cos[..., :modes_y] + with_sin[..., modes_y:],
            with_cos[..., modes_y:] - with_sin[..., :modes_y],
        ],
        axis=-1,
    )
    spec_grad = lax.psum_scatter(joined * forward_scale, "space", scatter_dimension=0, tiled=True)
    input_spec = spectral_backward(spec_grad, weights, modes_y)
    local_terms = weight_terms(spectrum, spec_grad, modes_y)
    grad_weights = lax.psum_scatter(local_terms, "dp", scatter_dimension=1, tiled=True)
    shard_piece = lax.all_gather(input_spec, "space", axis=0, tiled=True)
    cosines, sines = row_basis(shard_piece.shape[0], first_row, row_count, height)
    back_cos = jnp.einsum("kx,krcj->rcxj", cosines, shard_piece, precision=hp)
    back_sin = jnp.einsum("kx,krcj->rcxj", sines, shard_piece, precision=hp)
    joined = jnp.concatenate(
        [
            back_cos[..., :modes_y] - back_sin[..., modes_y:],
            back_cos[..., modes_y:] + back_sin[..., :modes_y],
        ],
        axis=-1,
    )
    inverse_scale = 1.0 / math.sqrt(local_modes * space_count * modes_y)
    grad_input = (jnp.einsum("rcxj,wj->rcxw", joined, basis, precision=hp) * inverse_scale).astype(
        jnp.bfloat16
    )
    return (grad_input, grad_weights)


def solution(mesh):
    placed = (
        P("dp", None, "space", None),
        P("space", "dp", None, None),
        P("space", None, None, None),
    )
    return jax.shard_map(
        body,
        mesh=mesh,
        in_specs=placed,
        out_specs=(P("dp", None, "space", None), P("space", "dp", None)),
        check_vma=False,
    )
```

profile of v0, /device:TPU:0, one launch (start us, length us, event | category | flops | bytes accessed | tf_op | source)
XLA Modules:
  0.0 120.1 jit_solution(17642633677702430916)
XLA Ops:
  7.2 0.0 copy-start
  7.2 0.0 reduce-scatter.3.cloned.1.call-start
  7.2 2.1 %sine_negate_fusion = (f32[1024,64]{1,0:T(8,128)S(1)}, f32[1024,64]{1,0:T(8,128)S(1)}) fusion(), kind=kLoop, calls=%fused_computation.28 | loop fusion | flops 983040 | bytes 524288 | tf_op jit(solution)/shard_map/neg | solution.py:14
  9.3 0.0 copy-done
  9.3 1.5 %fusion.3 = f32[24,32,128]{2,1,0:T(8,128)S(1)} fusion(bf16[1,24,32,1024]{3,2,1,0:T(8,128)(2,1)S(1)} %copy-done, f32[1024,64]{1,0:T(8,128)S(1)} %get-tuple-element.22, f32[1024,64]{1,0:T(8,128)S(1)} %get-tuple-element.23), kind=kOutput, calls=%fused_computation.13 | convolution fusion | flops 1208090624 | bytes 2490368 | tf_op jit(solution)/shard_map/rcxw,wj->rcxj/dot_general | solution.py:61
  10.8 1.0 convolution_bitcast_fusion
  11.8 0.0 copy-start.3
  11.8 1.0 convolution_bitcast_fusion.1
  12.8 0.5 slice_add_fusion
  13.3 1.2 maximum_multiply_fusion
  14.4 0.0 reduce-scatter.3.cloned.1.call-update
  14.4 0.0 reduce-scatter.5.cloned.1.call-start
  14.5 0.0 copy-done.3
  14.5 0.1 slice_bitcast_fusion.3
  14.6 28.8 %reduce-scatter.3.cloned.1.call-done = f32[16,1,24,128]{3,0,2,1:T(8,128)} async-done(((f32[64,1,24,128]{3,0,2,1:T(8,128)}), f32[16,1,24,128]{3,0,2,1:T(8,128)}) %reduce-scatter.3.cloned.1.call-update) | async-done | bytes 196624 | tf_op jit(solution)/shard_map/reduce_scatter | solution.py:75
  43.4 1.1 slice_bitcast_fusion
  44.5 0.1 copy.40
  44.6 0.1 copy.39
  44.7 10.0 %add_bitcast_fusion = (f32[16,24,24,64]{3,2,1,0:T(8,128)S(1)}, f32[16,24,24,64]{3,2,1,0:T(8,128)S(1)}, f32[16,64,24]{1,2,0:T(8,128)S(1)}, f32[16,64,24]{1,2,0:T(...) fusion(f32[16,64,24]{1,2,0:T(8,128)S(1)} %copy.40, f32[16,64,24]{1,2,0:T(8,128)S(1)} %copy.39, ...), kind=kLoop, calls=%fused_computation.6 | loop fusion | flops 8159232 | bytes 10223616 | tf_op jit(solution)/shard_map/add | solution.py:42
  54.7 3.4 %pad_maximum_fusion = f32[16,24,24,128]{3,2,1,0:T(8,128)} fusion(f32[16,24,24,64]{3,2,1,0:T(8,128)S(1)} %get-tuple-element.11, f32[16,24,24,64]{3,2,1,0:T(8,128)S(1)} %get-tuple-element.10), kind=kLoop, calls=%fused_computation | loop fusion | flops 1179648 | bytes 9437184 | tf_op jit(solution)/shard_map/concatenate | solution.py:48
  58.1 0.0 copy-start.1
  58.1 0.0 copy-start.2
  58.1 0.0 reduce-scatter.5.cloned.1.call-update
  58.1 0.9 copy-done.1
  59.0 0.1 copy-done.2
  59.1 0.1 fusion.17
  59.2 0.1 fusion.18
  59.3 0.1 pad_maximum_fusion.1
  59.4 11.3 %all_gather.3 = f32[64,1,24,128]{3,0,2,1:T(8,128)S(1)} all-gather(f32[16,1,24,128]{3,0,2,1:T(8,128)S(1)} %pad_maximum_fusion.1), channel_id=1, replica_groups=mesh['dp'=8,'space'=4] {'space'}, dimensions={0}, use_global_device_ids=true | all-gather | bytes 983040 | tf_op jit(solution)/shard_map/all_gather | solution.py:79
  70.7 0.7 convolution_bitcast_fusion.2
  71.4 0.7 convolution_bitcast_fusion.3
  72.1 0.3 slice_subtract_fusion.1
  72.4 3.9 %fusion.2 = bf16[1,24,32,1024]{3,2,1,0:T(8,128)(2,1)} fusion(f32[1,24,32,64]{3,2,1,0:T(8,128)S(1)} %get-tuple-element.13, f32[1,24,32,64]{3,2,1,0:T(8,128)S(1)} %get-tuple-element.12, f32[1024,64]{1,0:T(8,128)S(1)} %get-tuple-element.22, f32[1024,64]{1,0:T(8,128)S(1)} %get-tuple-element.23), kind=kOutput, calls=%fused_computation.10 | convolution fusion | flops 1209761792 | bytes 2490368 | tf_op jit(solution)/shard_map/rcxj,wj->rcxw/dot_general | solution.py:91
  76.3 36.9 %reduce-scatter.5.cloned.1.call-done = f32[16,72,128]{2,1,0:T(8,128)} async-done(((f32[16,576,128]{2,1,0:T(8,128)}), f32[16,72,128]{2,1,0:T(8,128)}) %reduce-scatter.5.cloned.1.call-update) | async-done | bytes 589840 | tf_op jit(solution)/shard_map/reduce_scatter | solution.py:78
  (1 shorter events, 0.0 us)
Async XLA Ops:
  7.2 2.2 %copy-start = (bf16[1,24,32,1024]{3,2,1,0:T(8,128)(2,1)S(1)}, bf16[1,24,32,1024]{3,2,1,0:T(8,128)(2,1)}, u32[]{:S(2)}) copy-start(bf16[1,24,32,1024]{3,2,1,0:T(8,128)(2,1)} %param.3) | copy-start | bytes 4718596
  7.2 36.2 %reduce-scatter.3.cloned.1.call-start = ((), (), s32[]{:S(2)}) async-start(), calls=%async_computation.2 | async-start | bytes 983040 | tf_op jit(solution)/shard_map/reduce_scatter | solution.py:75
  11.8 2.7 %copy-start.3 = (f32[16,1,24,128]{3,2,1,0:T(8,128)S(1)}, f32[16,1,24,128]{3,2,1,0:T(8,128)}, u32[]{:S(2)}) copy-start(f32[16,1,24,128]{3,2,1,0:T(8,128)} %param.4) | copy-start | bytes 589828
  14.4 98.8 %reduce-scatter.5.cloned.1.call-start = ((), (), s32[]{:S(2)}) async-start(), calls=%async_computation.3 | async-start | bytes 5308416 | tf_op jit(solution)/shard_map/reduce_scatter | solution.py:78
  58.1 0.9 copy-start.1
  58.1 1.0 copy-start.2
Sparse Core Ops, SparseCore 0:
  14.6 28.7 reduce-scatter.2
  58.2 54.9 reduce-scatter.4
where the time goes:
time: 120 us
  waiting for transfers between devices  65.7 us (55%)
  other arithmetic  17.6 us (15%)
  between operations  14.2 us (12%)
  blocking collectives  11.3 us (9%)
  matrix products  8.81 us (7%)
  local copies, waits for them, and re-layouts  2.38 us (2%)
    reduce_scatter x1, waiting for transfers between devices, body(): lax.psum_scatter(local_terms, 'dp', scatter_dimension=1, tiled=True)  36.9 us
    reduce_scatter x1, waiting for transfers between devices, body(): lax.psum_scatter(joined * forward_scale, 'space', scatter_dimension=0, ti...  28.8 us
    all_gather x1, blocking collectives, body(): shard_piece = lax.all_gather(input_spec, 'space', axis=0, tiled=True)  11.3 us
    add x1, other arithmetic, weight_terms(): jnp.einsum('kbcx,kbox->kcox', spec_re, grad_re, precision=hp)  10 us
    dot_general x1, matrix products, body(): jnp.einsum('rcxj,wj->rcxw', joined, basis, precision=hp) * inverse_scale  3.94 us
    concatenate x1, other arithmetic, weight_terms(): joined = jnp.concatenate([real_part, imag_part], axis=-1)  3.41 us
  transfers between devices with their start and end apart: 2, of which 2 were waited for; matrix products, arithmetic and copies ran while one was open for 5% of the time, Pallas kernels for 0%

commit v1 on v0

--- a/solution.py
+++ b/solution.py
@@ -1,9 +1,17 @@
+import functools
 import math
 
 import jax
 import jax.numpy as jnp
+import ml_dtypes
+import numpy as np
 from jax import lax
+from jax.experimental import pallas as pl
+from jax.experimental.pallas import tpu as pltpu
 from jax.sharding import PartitionSpec as P
+
+MESH = pl.DeviceIdType.MESH
+GROUP = 8
 
 
 def column_basis(col_count, modes_y):
@@ -49,7 +57,7 @@
     return joined.reshape(joined.shape[0], joined.shape[1] * joined.shape[2], joined.shape[3])
 
 
-def body(cotangent, spectrum, weights):
+def general_body(cotangent, spectrum, weights):
     hp = lax.Precision.HIGHEST
     space_count = lax.axis_size("space")
     raster_count, channels, row_count, col_count = cotangent.shape
@@ -94,12 +102,464 @@
     return (grad_input, grad_weights)
 
 
+def halves(table):
+    high = table.astype(ml_dtypes.bfloat16)
+    low = (table - high.astype(np.float64)).astype(ml_dtypes.bfloat16)
+    return high, low
+
+
+def tables(modes, modes_y, rows, cols, space):
+    height = rows * space
+    angle = 2.0 * np.pi * (np.outer(np.arange(cols), np.arange(modes_y)) % cols) / cols
+    high, low = halves(np.concatenate([np.cos(angle), -np.sin(angle)], axis=1))
+    into = np.concatenate([high, low], axis=1)
+    out_of = np.concatenate([high.T, high.T, low.T], axis=0)
+    angle = 2.0 * np.pi * (np.outer(np.arange(modes), np.arange(height)) % height) / height
+    cosines = np.cos(angle).reshape(modes, space, rows).transpose(1, 0, 2)
+    sines = np.sin(angle).reshape(modes, space, rows).transpose(1, 0, 2)
+    high, low = halves(np.concatenate([cosines, sines], axis=2) / math.sqrt(height * cols))
+    rows_in = np.concatenate([high, low, high], axis=2)
+    both = np.concatenate([cosines, sines], axis=1).transpose(0, 2, 1)
+    high, low = halves(both / math.sqrt(modes * modes_y))
+    rows_out = np.concatenate([high, low, high], axis=2)
+    return into, rows_in, rows_out, out_of
+
+
+def split(values):
+    high = values.astype(jnp.bfloat16)
+    low = (values - high.astype(jnp.float32)).astype(jnp.bfloat16)
+    return high, low
+
+
+def kernel(
+    dp, space,
+    cot_hbm, spec_hbm, w_hbm, into_hbm, rows_in_hbm, rows_out_hbm, out_of_hbm,
+    gin_ref, gw_ref,
+    cot, spec, w, into, rows_in, rows_out, out_of,
+    part, rs_in, gall, iall, sp_out, sp_in, a_rows, b_rows,
+    load_sem, rs_send, rs_recv, ag_send, ag_recv, sp_send, sp_recv,
+    up_send, down_send, sib_send, g_recv,
+):
+    me_d = lax.axis_index("dp")
+    me_s = lax.axis_index("space")
+    channels, rows, cols = cot.shape
+    local = w.shape[0]
+    modes = local * space
+    lanes = w.shape[3]
+    half = lanes // 2
+    own = channels // dp
+    groups = channels // GROUP
+
+    def at(d, s):
+        return {"dp": d, "space": s}
+
+    def partner_d(t):
+        return lax.rem(me_d + t, dp)
+
+    def partner_s(t):
+        return lax.rem(me_s + t, space)
+
+    def source_s(t):
+        return lax.rem(me_s + space - t, space)
+
+    barrier = pltpu.get_barrier_semaphore()
+    for t in range(1, dp):
+        pl.semaphore_signal(barrier, inc=1, device_id=at(partner_d(t), me_s), device_id_type=MESH)
+    for t in range(1, space):
+        pl.semaphore_signal(barrier, inc=1, device_id=at(me_d, partner_s(t)), device_id_type=MESH)
+
+    def load(n, src, dst):
+        copy = pltpu.make_async_copy(src, dst, load_sem.at[n])
+        copy.start()
+        return copy
+
+    l_into = load(0, into_hbm, into)
+    l_cot = []
+    for g in range(groups):
+        place = pl.ds(g * GROUP, GROUP)
+        l_cot.append(load(1 + g, cot_hbm.at[0, place], cot.at[place]))
+    n = 1 + groups
+    l_rows_in = load(n, rows_in_hbm.at[me_s], rows_in)
+    l_spec = load(n + 1, spec_hbm.at[:, 0], spec)
+    l_w = load(n + 2, w_hbm, w)
+    l_rows_out = load(n + 3, rows_out_hbm.at[me_s], rows_out)
+    l_out_of = load(n + 4, out_of_hbm, out_of)
+
+    lane = lax.broadcasted_iota(jnp.int32, (1, lanes), 1)
+    lower = lane < half
+    sign = jnp.where(lower, 1.0, -1.0).astype(jnp.float32)
+
+    def turn(values):
+        return pltpu.roll(values, half, values.ndim - 1)
+
+    def rs_copy(t, g):
+        there = partner_s(t)
+        place = pl.ds(g * GROUP, GROUP)
+        return pltpu.make_async_remote_copy(
+            part.at[pl.ds(there * local, local), place],
+            rs_in.at[t - 1, :, place],
+            rs_send.at[t - 1, g],
+            rs_recv.at[t - 1, g],
+            device_id=at(me_d, there),
+            device_id_type=MESH,
+        )
+
+    def sp_copy(t):
+        there = partner_d(t)
+        return pltpu.make_async_remote_copy(
+            sp_out.at[there],
+            sp_in.at[me_d],
+            sp_send.at[t],
+            sp_recv.at[t],
+            device_id=at(there, me_s),
+            device_id_type=MESH,
+        )
+
+    def sp_arrival(t):
+        source = lax.rem(me_d + dp - t, dp)
+        return pltpu.make_async_remote_copy(
+            sp_out.at[source],
+            sp_in.at[source],
+            sp_send.at[t],
+            sp_recv.at[t],
+            device_id=at(source, me_s),
+            device_id_type=MESH,
+        )
+
+    l_into.wait()
+    l_rows_in.wait()
+    for g in range(groups):
+        l_cot[g].wait()
+        block = cot[pl.ds(g * GROUP, GROUP)].reshape(GROUP * rows, cols)
+        both = jnp.dot(block, into[...], preferred_element_type=jnp.float32)
+        col = both[:, :lanes] + both[:, lanes:]
+        turned = turn(col) * sign
+        stacked = jnp.concatenate(
+            [
+                jnp.concatenate(
+                    [col[i * rows : (i + 1) * rows], turned[i * rows : (i + 1) * rows]], axis=0
+                )
+                for i in range(GROUP)
+            ],
+            axis=1,
+        )
+        high, low = split(stacked)
+        spectrum_part = jnp.dot(
+            rows_in[...],
+            jnp.concatenate([high, high, low], axis=0),
+            preferred_element_type=jnp.float32,
+        )
+        for i in range(GROUP):
+            part[:, g * GROUP + i, :] = spectrum_part[:, i * lanes : (i + 1) * lanes]
+        if g == 0:
+            pl.semaphore_wait(barrier, dp + space - 2)
+        for t in range(1, space):
+            rs_copy(t, g).start()
+
+    l_spec.wait()
+    for d in range(dp):
+        for k in range(local):
+            sp_out[d, k * own : (k + 1) * own, :] = spec[k, d * own : (d + 1) * own, :]
+    for t in range(1, dp):
+        sp_copy(t).start()
+    sp_in[me_d] = sp_out[me_d]
+    gw_ref[...] = jnp.zeros_like(gw_ref)
+
+    for t in range(1, space):
+        for g in range(groups):
+            rs_copy(t, g).wait_recv()
+
+    def gather_sum(k, carry):
+        total = part[me_s * local + k]
+        for t in range(1, space):
+            total = total + rs_in[t - 1, k]
+        gall[me_d, k] = total
+        return carry
+
+    lax.fori_loop(0, local, gather_sum, 0)
+
+    z, core = me_d // 2, lax.rem(me_d, 2)
+    nz = dp // 2
+
+    def g_copy(b, there, sem):
+        return pltpu.make_async_remote_copy(
+            gall.at[b],
+            gall.at[b],
+            sem.at[b],
+            g_recv.at[b],
+            device_id=at(there, me_s),
+            device_id_type=MESH,
+        )
+
+    def up(b):
+        return g_copy(b, me_d + 2, up_send)
+
+    def down(b):
+        return g_copy(b, me_d - 2, down_send)
+
+    def sibling(b):
+        return g_copy(b, me_d + 1 - 2 * core, sib_send)
+
+    @pl.when(z < nz - 1)
+    def _():
+        up(me_d).start()
+
+    @pl.when(z > 0)
+    def _():
+        down(me_d).start()
+
+    sibling(me_d).start()
+
+    parts = 2 if local % 2 == 0 else 1
+    size = local // parts
+
+    def ag_copy(t, h):
+        place = pl.ds(me_s * local + h * size, size)
+        return pltpu.make_async_remote_copy(
+            iall.at[place],
+            iall.at[place],
+            ag_send.at[t - 1, h],
+            ag_recv.at[t - 1, h],
+            device_id=at(me_d, partner_s(t)),
+            device_id_type=MESH,
+        )
+
+    def ag_arrival(t, h):
+        place = pl.ds(source_s(t) * local + h * size, size)
+        return pltpu.make_async_remote_copy(
+            iall.at[place],
+            iall.at[place],
+            ag_send.at[t - 1, h],
+            ag_recv.at[t - 1, h],
+            device_id=at(me_d, source_s(t)),
+            device_id_type=MESH,
+        )
+
+    def mix(k, carry):
+        grad = gall[me_d, k]
+        weight = w[k]
+        plain = jnp.sum(weight * grad[None], axis=1)
+        cross = jnp.sum(weight * turn(grad)[None], axis=1)
+        iall[me_s * local + k] = jnp.where(lower, plain + turn(plain), turn(cross) - cross)
+        return carry
+
+    l_w.wait()
+    for h in range(parts):
+        lax.fori_loop(h * size, (h + 1) * size, mix, 0)
+        for t in range(1, space):
+            ag_copy(t, h).start()
+
+    for t in range(1, dp):
+        sp_arrival(t).wait_recv()
+
+    def add_terms(b):
+        saved = sp_in[b]
+        a_rows[...] = jnp.where(lower, saved, turn(saved))
+        b_rows[...] = jnp.where(lower, turn(saved), -saved)
+
+        def one(k, carry):
+            grad = gall[b, k]
+            turned = turn(grad)
+            for c in range(own):
+                row = pl.ds(k * own + c, 1)
+                place = pl.ds(c * channels, channels)
+                gw_ref[k, place, :] += a_rows[row, :] * grad + b_rows[row, :] * turned
+            return carry
+
+        lax.fori_loop(0, local, one, 0)
+
+    add_terms(me_d)
+    g_copy(me_d + 1 - 2 * core, me_d, sib_send).wait_recv()
+    add_terms(me_d + 1 - 2 * core)
+
+    def step(t):
+        below, above = me_d - 2 * t, me_d + 2 * t
+
+        @pl.when(z >= t)
+        def _():
+            down(below).wait_recv()
+
+            @pl.when(z < nz - 1)
+            def _():
+                up(below).start()
+
+            sibling(below).start()
+
+        @pl.when(z + t < nz)
+        def _():
+            up(above).wait_recv()
+
+            @pl.when(z > 0)
+            def _():
+                down(above).start()
+
+            sibling(above).start()
+
+        @pl.when(z >= t)
+        def _():
+            add_terms(below)
+            other = below + 1 - 2 * core
+            sibling(other).wait_recv()
+            add_terms(other)
+
+        @pl.when(z + t < nz)
+        def _():
+            add_terms(above)
+            other = above + 1 - 2 * core
+            sibling(other).wait_recv()
+            add_terms(other)
+
+    def back_transform():
+        l_rows_out.wait()
+        l_out_of.wait()
+        for t in range(1, space):
+            for h in range(parts):
+                ag_arrival(t, h).wait_recv()
+        for g in range(groups):
+            mixed = jnp.concatenate(
+                [iall[:, g * GROUP + i, :] for i in range(GROUP)], axis=1
+            )
+            turned = jnp.concatenate(
+                [
+                    -sign * turn(mixed[:, i * lanes : (i + 1) * lanes])
+                    for i in range(GROUP)
+                ],
+                axis=1,
+            )
+            high, low = split(jnp.concatenate([mixed, turned], axis=0))
+            back = jnp.dot(
+                rows_out[...],
+                jnp.concatenate([high, high, low], axis=0),
+                preferred_element_type=jnp.float32,
+            )
+            back = jnp.concatenate(
+                [back[:, i * lanes : (i + 1) * lanes] for i in range(GROUP)], axis=0
+            )
+            high, low = split(back)
+            raster = jnp.dot(
+                jnp.concatenate([high, low, high], axis=1),
+                out_of[...],
+                preferred_element_type=jnp.float32,
+            )
+            gin_ref[0, pl.ds(g * GROUP, GROUP)] = raster.reshape(GROUP, rows, cols).astype(
+                jnp.bfloat16
+            )
+
+    for t in range(1, nz):
+        if t == nz - 1:
+            back_transform()
+        step(t)
+
+    for t in range(1, space):
+        for g in range(groups):
+            rs_copy(t, g).wait_send()
+        for h in range(parts):
+            ag_copy(t, h).wait_send()
+    for t in range(1, dp):
+        sp_copy(t).wait_send()
+    sibling(me_d).wait_send()
+
+    @pl.when(z < nz - 1)
+    def _():
+        up(me_d).wait_send()
+
+    @pl.when(z > 0)
+    def _():
+        down(me_d).wait_send()
+
+    for t in range(1, nz):
+
+        @pl.when(z >= t)
+        def _():
+            @pl.when(z < nz - 1)
+            def _():
+                up(me_d - 2 * t).wait_send()
+
+            sibling(me_d - 2 * t).wait_send()
+
+        @pl.when(z + t < nz)
+        def _():
+            @pl.when(z > 0)
+            def _():
+                down(me_d + 2 * t).wait_send()
+
+            sibling(me_d + 2 * t).wait_send()
+
+
+def fused_body(dp, space, cotangent, spectrum, weights):
+    _, channels, rows, cols = cotangent.shape
+    local, _, _, lanes = spectrum.shape
+    modes = local * space
+    own = channels // dp
+    groups = channels // GROUP
+    fixed = [jnp.asarray(t) for t in tables(modes, lanes // 2, rows, cols, space)]
+    into, rows_in, rows_out, out_of = fixed
+    f32 = jnp.float32
+    dma = pltpu.SemaphoreType.DMA
+    return pl.pallas_call(
+        functools.partial(kernel, dp, space),
+        out_shape=(
+            jax.ShapeDtypeStruct(cotangent.shape, jnp.bfloat16),
+            jax.ShapeDtypeStruct((local, own * channels, lanes), f32),
+        ),
+        in_specs=[pl.BlockSpec(memory_space=pl.ANY)] * 7,
+        out_specs=[pl.BlockSpec(memory_space=pltpu.VMEM)] * 2,
+        scratch_shapes=[
+            pltpu.VMEM((channels, rows, cols), jnp.bfloat16),
+            pltpu.VMEM((local, channels, lanes), f32),
+            pltpu.VMEM(weights.shape, f32),
+            pltpu.VMEM(into.shape, jnp.bfloat16),
+            pltpu.VMEM(rows_in.shape[1:], jnp.bfloat16),
+            pltpu.VMEM(rows_out.shape[1:], jnp.bfloat16),
+            pltpu.VMEM(out_of.shape, jnp.bfloat16),
+            pltpu.VMEM((modes, channels, lanes), f32),
+            pltpu.VMEM((space - 1, local, channels, lanes), f32),
+            pltpu.VMEM((dp, local, channels, lanes), f32),
+            pltpu.VMEM((modes, channels, lanes), f32),
+            pltpu.VMEM((dp, local * own, lanes), f32),
+            pltpu.VMEM((dp, local * own, lanes), f32),
+            pltpu.VMEM((local * own, lanes), f32),
+            pltpu.VMEM((local * own, lanes), f32),
+            dma((groups + 6,)),
+            dma((space - 1, groups)),
+            dma((space - 1, groups)),
+            dma((space - 1, 2)),
+            dma((space - 1, 2)),
+            dma((dp,)),
+            dma((dp,)),
+            dma((dp,)),
+            dma((dp,)),
+            dma((dp,)),
+            dma((dp,)),
+        ],
+        compiler_params=pltpu.CompilerParams(
+            collective_id=0, has_side_effects=True, vmem_limit_bytes=48 * 1024 * 1024
+        ),
+    )(cotangent, spectrum, weights, into, rows_in, rows_out, out_of)
+
+
 def solution(mesh):
     placed = (
         P("dp", None, "space", None),
         P("space", "dp", None, None),
         P("space", None, None, None),
     )
+    dp, space = mesh.shape["dp"], mesh.shape["space"]
+
+    def body(cotangent, spectrum, weights):
+        rasters, channels, rows, _ = cotangent.shape
+        whole_rows = (
+            rasters == 1
+            and dp % 2 == 0
+            and channels % dp == 0
+            and channels % GROUP == 0
+            and rows % 16 == 0
+            and (spectrum.shape[0] * (channels // dp)) % 8 == 0
+        )
+        if whole_rows:
+            return fused_body(dp, space, cotangent, spectrum, weights)
+        return general_body(cotangent, spectrum, weights)
+
     return jax.shard_map(
         body,
         mesh=mesh,

time: 120 us -> 45.7 us (0.38)
  the two profiles are of different devices: /device:TPU:0 before, /device:TPU:1 now
where the time goes in v1:
time: 45.7 us; the launch traced here: 45.1 us
  Pallas kernels  36.2 us (79%)
  local copies, waits for them, and re-layouts  8.26 us (18%)
  between operations  0.65 us (1%)
    pallas_call x1, Pallas kernels, fused_body(): pl.pallas_call(functools.partial(kernel, dp, space), out_shape=(jax.Shape...  36.2 us
    unnamed x14, local copies, waits for them, and re-layouts  8.26 us

profile of v1, /device:TPU:1, one launch (start us, length us, event | category | flops | bytes accessed | tf_op | source)
XLA Modules:
  0.0 45.1 jit_solution(10110162865710570852)
XLA Ops:
  0.6 0.0 copy-start
  0.6 1.4 %copy-done = bf16[1,24,32,1024]{3,2,1,0:T(8,128)(2,1)S(1)} copy-done((bf16[1,24,32,1024]{3,2,1,0:T(8,128)(2,1)S(1)}, bf16[1,24,32,1024]{3,2,1,0:T(8,128)(2,1)}, u32[]{:S(2)}) %copy-start) | copy-done | bytes 1572888
  2.0 0.0 copy-start.1
  2.0 1.1 %copy-done.1 = bf16[384,1024]{1,0:T(8,128)(2,1)S(1)} copy-done((bf16[384,1024]{1,0:T(8,128)(2,1)S(1)}, bf16[384,1024]{1,0:T(8,128)(2,1)}, u32[]{:S(2)}) %copy-start.1) | copy-done | bytes 786456
  3.2 0.0 copy-start.2
  3.2 1.0 %copy-done.2 = bf16[1024,256]{1,0:T(8,128)(2,1)S(1)} copy-done((bf16[1024,256]{1,0:T(8,128)(2,1)S(1)}, bf16[1024,256]{1,0:T(8,128)(2,1)}, u32[]{:S(2)}) %copy-start.2) | copy-done | bytes 524312
  4.2 0.0 copy-start.3
  4.2 0.9 %copy-done.3 = f32[16,1,24,128]{3,2,1,0:T(8,128)S(1)} copy-done((f32[16,1,24,128]{3,2,1,0:T(8,128)S(1)}, f32[16,1,24,128]{3,2,1,0:T(8,128)}, u32[]{:S(2)}) %copy-start.3) | copy-done | bytes 196632
  5.1 0.0 copy-start.4
  5.1 0.9 %copy-done.4 = bf16[4,64,192]{2,1,0:T(8,128)(2,1)S(1)} copy-done((bf16[4,64,192]{2,1,0:T(8,128)(2,1)S(1)}, bf16[4,64,192]{2,1,0:T(8,128)(2,1)}, u32[]{:S(2)}) %copy-start.4) | copy-done | bytes 98328
  6.0 0.0 copy-start.5
  6.0 0.9 %copy-done.5 = bf16[4,32,384]{2,1,0:T(8,128)(2,1)S(1)} copy-done((bf16[4,32,384]{2,1,0:T(8,128)(2,1)S(1)}, bf16[4,32,384]{2,1,0:T(8,128)(2,1)}, u32[]{:S(2)}) %copy-start.5) | copy-done | bytes 98328
  6.9 36.2 %shard_map.86 = (bf16[1,24,32,1024]{3,2,1,0:T(8,128)(2,1)S(1)}, f32[16,72,128]{2,1,0:T(8,128)S(1)}) custom-call(bf16[1,24,32,1024]{3,2,1,0:T(8,128)(2,1)S(1)} %copy-done, f32[16,1,24,128]{3,2,1,0:T(8,128)S(1)} %copy-done.3, f32[16,24,24,128]{3,2,1,0:T(8,128)} %w_hbm.1, bf16[1024,256]{1,0:T(8,128)(2,1)S(1)} %copy-done.2, bf16[4,64,192]{2,1,0:T(8,128)(2,1)S(1)} %copy-done.4, ...), custom_call_target="tpu_custom_call" | custom-call | tf_op jit(solution)/shard_map/pallas_call | solution.py:499
  43.2 1.1 %copy.11 = bf16[1,24,32,1024]{3,2,1,0:T(8,128)(2,1)} copy(bf16[1,24,32,1024]{3,2,1,0:T(8,128)(2,1)S(1)} %get-tuple-element.4) | data formatting | bytes 3145728
  44.3 0.8 %copy.12 = f32[16,72,128]{2,1,0:T(8,128)} copy(f32[16,72,128]{2,1,0:T(8,128)S(1)} %get-tuple-element.5) | data formatting | bytes 1179648
Async XLA Ops:
  0.6 1.4 %copy-start = (bf16[1,24,32,1024]{3,2,1,0:T(8,128)(2,1)S(1)}, bf16[1,24,32,1024]{3,2,1,0:T(8,128)(2,1)}, u32[]{:S(2)}) copy-start(bf16[1,24,32,1024]{3,2,1,0:T(8,128)(2,1)} %cot_hbm.1) | copy-start | bytes 4718596
  2.0 1.1 %copy-start.1 = (bf16[384,1024]{1,0:T(8,128)(2,1)S(1)}, bf16[384,1024]{1,0:T(8,128)(2,1)}, u32[]{:S(2)}) copy-start(bf16[384,1024]{1,0:T(8,128)(2,1)} %constant.11.clone.out_of_hbm) | copy-start | bytes 2359300
  3.2 1.0 %copy-start.2 = (bf16[1024,256]{1,0:T(8,128)(2,1)S(1)}, bf16[1024,256]{1,0:T(8,128)(2,1)}, u32[]{:S(2)}) copy-start(bf16[1024,256]{1,0:T(8,128)(2,1)} %constant.8.clone.into_hbm) | copy-start | bytes 1572868
  4.2 0.9 %copy-start.3 = (f32[16,1,24,128]{3,2,1,0:T(8,128)S(1)}, f32[16,1,24,128]{3,2,1,0:T(8,128)}, u32[]{:S(2)}) copy-start(f32[16,1,24,128]{3,2,1,0:T(8,128)} %spec_hbm.1) | copy-start | bytes 589828
  5.1 0.9 %copy-start.4 = (bf16[4,64,192]{2,1,0:T(8,128)(2,1)S(1)}, bf16[4,64,192]{2,1,0:T(8,128)(2,1)}, u32[]{:S(2)}) copy-start(bf16[4,64,192]{2,1,0:T(8,128)(2,1)} %constant.9.clone.rows_in_hbm) | copy-start | bytes 294916
  6.0 0.9 %copy-start.5 = (bf16[4,32,384]{2,1,0:T(8,128)(2,1)S(1)}, bf16[4,32,384]{2,1,0:T(8,128)(2,1)}, u32[]{:S(2)}) copy-start(bf16[4,32,384]{2,1,0:T(8,128)(2,1)} %constant.10.clone.rows_out_hbm) | copy-start | bytes 294916

commit v2 on v1

--- a/solution.py
+++ b/solution.py
@@ -119,9 +119,11 @@
     sines = np.sin(angle).reshape(modes, space, rows).transpose(1, 0, 2)
     high, low = halves(np.concatenate([cosines, sines], axis=2) / math.sqrt(height * cols))
     rows_in = np.concatenate([high, low, high], axis=2)
-    both = np.concatenate([cosines, sines], axis=1).transpose(0, 2, 1)
+    local = modes // space
+    order = np.arange(modes).reshape(space, 2, local // 2).transpose(1, 0, 2).reshape(2, -1)
+    both = np.concatenate([cosines[:, order], sines[:, order]], axis=2).transpose(0, 1, 3, 2)
     high, low = halves(both / math.sqrt(modes * modes_y))
-    rows_out = np.concatenate([high, low, high], axis=2)
+    rows_out = np.concatenate([high, low, high], axis=3)
     return into, rows_in, rows_out, out_of
 
 
@@ -134,10 +136,10 @@
 def kernel(
     dp, space,
     cot_hbm, spec_hbm, w_hbm, into_hbm, rows_in_hbm, rows_out_hbm, out_of_hbm,
-    gin_ref, gw_ref,
-    cot, spec, w, into, rows_in, rows_out, out_of,
-    part, rs_in, gall, iall, sp_out, sp_in, a_rows, b_rows,
-    load_sem, rs_send, rs_recv, ag_send, ag_recv, sp_send, sp_recv,
+    gin_hbm, gw_hbm,
+    gin_ref, gw_ref, cot, spec, w, into, rows_in, rows_out, out_of,
+    part, rs_in, gall, iall, back_sum, sp_out, sp_in, a_rows, b_rows,
+    load_sem, store_sem, rs_send, rs_recv, ag_send, ag_recv, sp_send, sp_recv,
     up_send, down_send, sib_send, g_recv,
 ):
     me_d = lax.axis_index("dp")
@@ -192,14 +194,19 @@
     def turn(values):
         return pltpu.roll(values, half, values.ndim - 1)
 
-    def rs_copy(t, g):
+    size = local // 2
+
+    def rs_copy(t, piece):
         there = partner_s(t)
-        place = pl.ds(g * GROUP, GROUP)
+        if piece < groups:
+            first, place = 0, pl.ds(piece * GROUP, GROUP)
+        else:
+            first, place = size, pl.ds(0, channels)
         return pltpu.make_async_remote_copy(
-            part.at[pl.ds(there * local, local), place],
-            rs_in.at[t - 1, :, place],
-            rs_send.at[t - 1, g],
-            rs_recv.at[t - 1, g],
+            part.at[pl.ds(there * local + first, size), place],
+            rs_in.at[t - 1, pl.ds(first, size), place],
+            rs_send.at[t - 1, piece],
+            rs_recv.at[t - 1, piece],
             device_id=at(me_d, there),
             device_id_type=MESH,
         )
@@ -255,6 +262,8 @@
             pl.semaphore_wait(barrier, dp + space - 2)
         for t in range(1, space):
             rs_copy(t, g).start()
+    for t in range(1, space):
+        rs_copy(t, groups).start()
 
     l_spec.wait()
     for d in range(dp):
@@ -265,59 +274,74 @@
     sp_in[me_d] = sp_out[me_d]
     gw_ref[...] = jnp.zeros_like(gw_ref)
 
-    for t in range(1, space):
-        for g in range(groups):
-            rs_copy(t, g).wait_recv()
-
-    def gather_sum(k, carry):
-        total = part[me_s * local + k]
-        for t in range(1, space):
-            total = total + rs_in[t - 1, k]
-        gall[me_d, k] = total
-        return carry
-
-    lax.fori_loop(0, local, gather_sum, 0)
-
     z, core = me_d // 2, lax.rem(me_d, 2)
     nz = dp // 2
-
-    def g_copy(b, there, sem):
+    twin = 1 - 2 * core
+
+    def g_copy(b, h, there, sem):
+        place = pl.ds(h * size, size)
         return pltpu.make_async_remote_copy(
-            gall.at[b],
-            gall.at[b],
-            sem.at[b],
-            g_recv.at[b],
+            gall.at[b, place],
+            gall.at[b, place],
+            sem.at[b, h],
+            g_recv.at[b, h],
             device_id=at(there, me_s),
             device_id_type=MESH,
         )
 
-    def up(b):
-        return g_copy(b, me_d + 2, up_send)
-
-    def down(b):
-        return g_copy(b, me_d - 2, down_send)
-
-    def sibling(b):
-        return g_copy(b, me_d + 1 - 2 * core, sib_send)
-
-    @pl.when(z < nz - 1)
-    def _():
-        up(me_d).start()
-
-    @pl.when(z > 0)
-    def _():
-        down(me_d).start()
-
-    sibling(me_d).start()
-
-    parts = 2 if local % 2 == 0 else 1
-    size = local // parts
+    def up(b, h):
+        return g_copy(b, h, me_d + 2, up_send)
+
+    def down(b, h):
+        return g_copy(b, h, me_d - 2, down_send)
+
+    def sibling(b, h):
+        return g_copy(b, h, me_d + twin, sib_send)
+
+    def own_sends(h, act):
+        @pl.when(z < nz - 1)
+        def _():
+            act(up(me_d, h))
+
+        @pl.when(z > 0)
+        def _():
+            act(down(me_d, h))
+
+        act(sibling(me_d, h))
+
+    def passed_on(t, h, act, arrive):
+        @pl.when(z >= t)
+        def _():
+            below = me_d - 2 * t
+            if arrive:
+                down(below, h).wait_recv()
+
+            @pl.when(z < nz - 1)
+            def _():
+                act(up(below, h))
+
+            act(sibling(below, h))
+
+        @pl.when(z + t < nz)
+        def _():
+            above = me_d + 2 * t
+            if arrive:
+                up(above, h).wait_recv()
+
+            @pl.when(z > 0)
+            def _():
+                act(down(above, h))
+
+            act(sibling(above, h))
+
+    def forward(t, h):
+        passed_on(t, h, lambda copy: copy.start(), True)
 
     def ag_copy(t, h):
-        place = pl.ds(me_s * local + h * size, size)
+        place = pl.ds(me_s * size, size)
         return pltpu.make_async_remote_copy(
-            iall.at[place],
-            iall.at[place],
+            iall.at[h, place],
+            iall.at[h, place],
             ag_send.at[t - 1, h],
             ag_recv.at[t - 1, h],
             device_id=at(me_d, partner_s(t)),
@@ -325,165 +349,178 @@
         )
 
     def ag_arrival(t, h):
-        place = pl.ds(source_s(t) * local + h * size, size)
+        place = pl.ds(source_s(t) * size, size)
         return pltpu.make_async_remote_copy(
-            iall.at[place],
-            iall.at[place],
+            iall.at[h, place],
+            iall.at[h, place],
             ag_send.at[t - 1, h],
             ag_recv.at[t - 1, h],
             device_id=at(me_d, source_s(t)),
             device_id_type=MESH,
         )
 
-    def mix(k, carry):
-        grad = gall[me_d, k]
-        weight = w[k]
-        plain = jnp.sum(weight * grad[None], axis=1)
-        cross = jnp.sum(weight * turn(grad)[None], axis=1)
-        iall[me_s * local + k] = jnp.where(lower, plain + turn(plain), turn(cross) - cross)
-        return carry
-
-    l_w.wait()
-    for h in range(parts):
+    def sum_and_mix(h):
+        for t in range(1, space):
+            for piece in range(groups) if h == 0 else (groups,):
+                rs_copy(t, piece).wait_recv()
+
+        def gather_sum(k, carry):
+            total = part[me_s * local + k]
+            for t in range(1, space):
+                total = total + rs_in[t - 1, k]
+            gall[me_d, k] = total
+            return carry
+
+        lax.fori_loop(h * size, (h + 1) * size, gather_sum, 0)
+        own_sends(h, lambda copy: copy.start())
+        if h == 0:
+            l_w.wait()
+
+        def mix(k, carry):
+            grad = gall[me_d, k]
+            weight = w[k]
+            plain = jnp.sum(weight * grad[None], axis=1)
+            cross = jnp.sum(weight * turn(grad)[None], axis=1)
+            mixed = jnp.where(lower, plain + turn(plain), turn(cross) - cross)
+            iall[h, me_s * size + k - h * size] = mixed
+            return carry
+
         lax.fori_loop(h * size, (h + 1) * size, mix, 0)
         for t in range(1, space):
             ag_copy(t, h).start()
 
-    for t in range(1, dp):
-        sp_arrival(t).wait_recv()
-
-    def add_terms(b):
+    def rows_of(b):
         saved = sp_in[b]
-        a_rows[...] = jnp.where(lower, saved, turn(saved))
-        b_rows[...] = jnp.where(lower, turn(saved), -saved)
-
+        a_rows[b] = jnp.where(lower, saved, turn(saved))
+        b_rows[b] = jnp.where(lower, turn(saved), -saved)
+
+    def add_terms(b, h):
         def one(k, carry):
             grad = gall[b, k]
             turned = turn(grad)
             for c in range(own):
                 row = pl.ds(k * own + c, 1)
                 place = pl.ds(c * channels, channels)
-                gw_ref[k, place, :] += a_rows[row, :] * grad + b_rows[row, :] * turned
+                gw_ref[k, place, :] += a_rows[b, row, :] * grad + b_rows[b, row, :] * turned
             return carry
 
-        lax.fori_loop(0, local, one, 0)
-
-    add_terms(me_d)
-    g_copy(me_d + 1 - 2 * core, me_d, sib_send).wait_recv()
-    add_terms(me_d + 1 - 2 * core)
-
-    def step(t):
-        below, above = me_d - 2 * t, me_d + 2 * t
-
+        lax.fori_loop(h * size, (h + 1) * size, one, 0)
+
+    def pair_terms(b, h):
+        add_terms(b, h)
+        sibling(b + twin, h).wait_recv()
+        add_terms(b + twin, h)
+
+    def terms(t, h):
         @pl.when(z >= t)
         def _():
-            down(below).wait_recv()
-
-            @pl.when(z < nz - 1)
-            def _():
-                up(below).start()
-
-            sibling(below).start()
+            pair_terms(me_d - 2 * t, h)
 
         @pl.when(z + t < nz)
         def _():
-            up(above).wait_recv()
-
-            @pl.when(z > 0)
-            def _():
-                down(above).start()
-
-            sibling(above).start()
-
-        @pl.when(z >= t)
-        def _():
-            add_terms(below)
-            other = below + 1 - 2 * core
-            sibling(other).wait_recv()
-            add_terms(other)
-
-        @pl.when(z + t < nz)
-        def _():
-            add_terms(above)
-            other = above + 1 - 2 * core
-            sibling(other).wait_recv()
-            add_terms(other)
-
-    def back_transform():
-        l_rows_out.wait()
-        l_out_of.wait()
+            pair_terms(me_d + 2 * t, h)
+
+    def rows_back(h):
         for t in range(1, space):
-            for h in range(parts):
-                ag_arrival(t, h).wait_recv()
+            ag_arrival(t, h).wait_recv()
         for g in range(groups):
-            mixed = jnp.concatenate(
-                [iall[:, g * GROUP + i, :] for i in range(GROUP)], axis=1
-            )
+            mixed = jnp.concatenate([iall[h, :, g * GROUP + i, :] for i in range(GROUP)], axis=1)
             turned = jnp.concatenate(
-                [
-                    -sign * turn(mixed[:, i * lanes : (i + 1) * lanes])
-                    for i in range(GROUP)
-                ],
+                [-sign * turn(mixed[:, i * lanes : (i + 1) * lanes]) for i in range(GROUP)],
                 axis=1,
             )
             high, low = split(jnp.concatenate([mixed, turned], axis=0))
-            back = jnp.dot(
-                rows_out[...],
+            found = jnp.dot(
+                rows_out[h],
                 jnp.concatenate([high, high, low], axis=0),
                 preferred_element_type=jnp.float32,
             )
-            back = jnp.concatenate(
-                [back[:, i * lanes : (i + 1) * lanes] for i in range(GROUP)], axis=0
-            )
-            high, low = split(back)
-            raster = jnp.dot(
-                jnp.concatenate([high, low, high], axis=1),
-                out_of[...],
-                preferred_element_type=jnp.float32,
-            )
-            gin_ref[0, pl.ds(g * GROUP, GROUP)] = raster.reshape(GROUP, rows, cols).astype(
-                jnp.bfloat16
-            )
-
-    for t in range(1, nz):
-        if t == nz - 1:
-            back_transform()
-        step(t)
+            place = pl.ds(g * GROUP * lanes, GROUP * lanes)
+            if h == 0:
+                back_sum[:, place] = found
+            else:
+                columns_back(g, back_sum[:, place] + found)
+
+    def gin_store(g):
+        place = pl.ds(g * GROUP, GROUP)
+        return pltpu.make_async_copy(gin_ref.at[place], gin_hbm.at[0, place], store_sem.at[g])
+
+    def gw_store(h):
+        place = pl.ds(h * size, size)
+        return pltpu.make_async_copy(
+            gw_ref.at[place], gw_hbm.at[place], store_sem.at[groups + h]
+        )
+
+    def columns_back(g, back):
+        back = jnp.concatenate(
+            [back[:, i * lanes : (i + 1) * lanes] for i in range(GROUP)], axis=0
+        )
+        high, low = split(back)
+        raster = jnp.dot(
+            jnp.concatenate([high, low, high], axis=1),
+            out_of[...],
+            preferred_element_type=jnp.float32,
+        )
+        gin_ref[pl.ds(g * GROUP, GROUP)] = raster.reshape(GROUP, rows, cols).astype(
+            jnp.bfloat16
+        )
+        gin_store(g).start()
+
+    sum_and_mix(0)
+    forward(1, 0)
+    for t in range(1, dp):
+        sp_arrival(t).wait_recv()
+    for b in range(dp):
+        rows_of(b)
+    sum_and_mix(1)
+    if nz > 2:
+        forward(2, 0)
+    pair_terms(me_d, 0)
+    forward(1, 1)
+    pair_terms(me_d, 1)
+    terms(1, 0)
+    if nz > 3:
+        forward(3, 0)
+    if nz > 2:
+        forward(2, 1)
+    l_rows_out.wait()
+    rows_back(0)
+    terms(1, 1)
+    if nz > 2:
+        terms(2, 0)
+    l_out_of.wait()
+    rows_back(1)
+    if nz > 2:
+        terms(2, 1)
+    if nz > 3:
+        terms(3, 0)
+        forward(3, 1)
+        terms(3, 1)
+    for t in range(4, nz):
+        for h in range(2):
+            forward(t, h)
+            terms(t, h)
+    for h in range(2):
+        gw_store(h).start()
+
+    def leave(copy):
+        copy.wait_send()
 
     for t in range(1, space):
-        for g in range(groups):
-            rs_copy(t, g).wait_send()
-        for h in range(parts):
+        for piece in range(groups + 1):
+            rs_copy(t, piece).wait_send()
+        for h in range(2):
             ag_copy(t, h).wait_send()
     for t in range(1, dp):
         sp_copy(t).wait_send()
-    sibling(me_d).wait_send()
-
-    @pl.when(z < nz - 1)
-    def _():
-        up(me_d).wait_send()
-
-    @pl.when(z > 0)
-    def _():
-        down(me_d).wait_send()
-
-    for t in range(1, nz):
-
-        @pl.when(z >= t)
-        def _():
-            @pl.when(z < nz - 1)
-            def _():
-                up(me_d - 2 * t).wait_send()
-
-            sibling(me_d - 2 * t).wait_send()
-
-        @pl.when(z + t < nz)
-        def _():
-            @pl.when(z > 0)
-            def _():
-                down(me_d + 2 * t).wait_send()
-
-            sibling(me_d + 2 * t).wait_send()
+    for h in range(2):
+        own_sends(h, leave)
+        for t in range(1, nz):
+            passed_on(t, h, leave, False)
+    for g in range(groups):
+        gin_store(g).wait()
+    for h in range(2):
+        gw_store(h).wait()
 
 
 def fused_body(dp, space, cotangent, spectrum, weights):
@@ -503,8 +540,10 @@
             jax.ShapeDtypeStruct((local, own * channels, lanes), f32),
         ),
         in_specs=[pl.BlockSpec(memory_space=pl.ANY)] * 7,
-        out_specs=[pl.BlockSpec(memory_space=pltpu.VMEM)] * 2,
+        out_specs=[pl.BlockSpec(memory_space=pl.ANY)] * 2,
         scratch_shapes=[
+            pltpu.VMEM((channels, rows, cols), jnp.bfloat16),
+            pltpu.VMEM((local, own * channels, lanes), f32),
             pltpu.VMEM((channels, rows, cols), jnp.bfloat16),
             pltpu.VMEM((local, channels, lanes), f32),
             pltpu.VMEM(weights.shape, f32),
@@ -515,25 +554,27 @@
             pltpu.VMEM((modes, channels, lanes), f32),
             pltpu.VMEM((space - 1, local, channels, lanes), f32),
             pltpu.VMEM((dp, local, channels, lanes), f32),
-            pltpu.VMEM((modes, channels, lanes), f32),
+            pltpu.VMEM((2, modes // 2, channels, lanes), f32),
+            pltpu.VMEM((rows, channels * lanes), f32),
             pltpu.VMEM((dp, local * own, lanes), f32),
             pltpu.VMEM((dp, local * own, lanes), f32),
-            pltpu.VMEM((local * own, lanes), f32),
-            pltpu.VMEM((local * own, lanes), f32),
+            pltpu.VMEM((dp, local * own, lanes), f32),
+            pltpu.VMEM((dp, local * own, lanes), f32),
             dma((groups + 6,)),
-            dma((space - 1, groups)),
-            dma((space - 1, groups)),
+            dma((groups + 2,)),
+            dma((space - 1, groups + 1)),
+            dma((space - 1, groups + 1)),
             dma((space - 1, 2)),
             dma((space - 1, 2)),
             dma((dp,)),
             dma((dp,)),
-            dma((dp,)),
-            dma((dp,)),
-            dma((dp,)),
-            dma((dp,)),
+            dma((dp, 2)),
+            dma((dp, 2)),
+            dma((dp, 2)),
+            dma((dp, 2)),
         ],
         compiler_params=pltpu.CompilerParams(
-            collective_id=0, has_side_effects=True, vmem_limit_bytes=48 * 1024 * 1024
+            collective_id=0, has_side_effects=True, vmem_limit_bytes=62 * 1024 * 1024
         ),
     )(cotangent, spectrum, weights, into, rows_in, rows_out, out_of)
 
@@ -553,6 +594,7 @@
             and dp % 2 == 0
             and channels % dp == 0
             and channels % GROUP == 0
+            and spectrum.shape[0] % 2 == 0
             and rows % 16 == 0
             and (spectrum.shape[0] * (channels // dp)) % 8 == 0
         )

time: 45.7 us -> 41.6 us (0.910)
  local copies, waits for them, and re-layouts: 8.26 us -> 3.62 us
  Pallas kernels: 36.2 us -> 37.2 us
    unnamed x14 -> x4, local copies, waits for them, and re-layouts: 8.26 us -> 3.62 us
    pallas_call x1, Pallas kernels: 36.2 us -> 37.2 us  [fused_body(): pl.pallas_call(functools.partial(kernel, dp, space), out_shape=(jax.Shape...]
where the time goes in v2:
time: 41.6 us; the launch traced here: 41.4 us
  Pallas kernels  37.2 us (89%)
  local copies, waits for them, and re-layouts  3.62 us (9%)
  between operations  0.65 us (2%)
    pallas_call x1, Pallas kernels, fused_body(): pl.pallas_call(functools.partial(kernel, dp, space), out_shape=(jax.Shape...  37.2 us
    unnamed x4, local copies, waits for them, and re-layouts  3.62 us

profile of v2, /device:TPU:1, one launch (start us, length us, event | category | flops | bytes accessed | tf_op | source)
XLA Modules:
  0.0 41.4 jit_solution(14594878279493892381)
XLA Ops:
  0.6 37.2 %shard_map.86 = (bf16[1,24,32,1024]{3,2,1,0:T(8,128)(2,1)}, f32[16,72,128]{2,1,0:T(8,128)}) custom-call(bf16[1,24,32,1024]{3,2,1,0:T(8,128)(2,1)} %cot_hbm.1, f32[16,1,24,128]{3,2,1,0:T(8,128)} %spec_hbm.1, f32[16,24,24,128]{3,2,1,0:T(8,128)} %w_hbm.1, bf16[1024,256]{1,0:T(8,128)(2,1)} %constant.8.clone.into_hbm, ...), custom_call_target="tpu_custom_call" | custom-call | tf_op jit(solution)/shard_map/pallas_call | solution.py:536
  37.8 0.0 copy-start
  37.8 2.8 %copy.11 = bf16[1,24,32,1024]{3,2,1,0:T(8,128)(2,1)} copy(bf16[1,24,32,1024]{3,2,1,0:T(8,128)(2,1)} %get-tuple-element.4) | data formatting | bytes 3145728
  40.6 0.0 copy-done
  40.6 0.8 %copy.12 = f32[16,72,128]{2,1,0:T(8,128)} copy(f32[16,72,128]{2,1,0:T(8,128)S(1)} %copy-done) | data formatting | bytes 1179648
Async XLA Ops:
  37.8 2.8 %copy-start = (f32[16,72,128]{2,1,0:T(8,128)S(1)}, f32[16,72,128]{2,1,0:T(8,128)}, u32[]{:S(2)}) copy-start(f32[16,72,128]{2,1,0:T(8,128)} %get-tuple-element.5) | copy-start | bytes 1769476

commit v3 on v2

--- a/solution.py
+++ b/solution.py
@@ -371,7 +371,7 @@
             gall[me_d, k] = total
             return carry
 
-        lax.fori_loop(h * size, (h + 1) * size, gather_sum, 0)
+        lax.fori_loop(h * size, (h + 1) * size, gather_sum, 0, unroll=True)
         own_sends(h, lambda copy: copy.start())
         if h == 0:
             l_w.wait()
@@ -385,7 +385,7 @@
             iall[h, me_s * size + k - h * size] = mixed
             return carry
 
-        lax.fori_loop(h * size, (h + 1) * size, mix, 0)
+        lax.fori_loop(h * size, (h + 1) * size, mix, 0, unroll=True)
         for t in range(1, space):
             ag_copy(t, h).start()
 
@@ -394,22 +394,24 @@
         a_rows[b] = jnp.where(lower, saved, turn(saved))
         b_rows[b] = jnp.where(lower, turn(saved), -saved)
 
-    def add_terms(b, h):
+    def add_terms(blocks, h):
         def one(k, carry):
-            grad = gall[b, k]
-            turned = turn(grad)
+            grads = [gall[b, k] for b in blocks]
+            turned = [turn(grad) for grad in grads]
             for c in range(own):
                 row = pl.ds(k * own + c, 1)
                 place = pl.ds(c * channels, channels)
-                gw_ref[k, place, :] += a_rows[b, row, :] * grad + b_rows[b, row, :] * turned
+                total = gw_ref[k, place, :]
+                for b, grad, other in zip(blocks, grads, turned):
+                    total = total + (a_rows[b, row, :] * grad + b_rows[b, row, :] * other)
+                gw_ref[k, place, :] = total
             return carry
 
-        lax.fori_loop(h * size, (h + 1) * size, one, 0)
+        lax.fori_loop(h * size, (h + 1) * size, one, 0, unroll=True)
 
     def pair_terms(b, h):
-        add_terms(b, h)
         sibling(b + twin, h).wait_recv()
-        add_terms(b + twin, h)
+        add_terms((b, b + twin), h)
 
     def terms(t, h):
         @pl.when(z >= t)

time: 41.6 us -> 36.8 us (0.88)
  Pallas kernels: 37.2 us -> 32.4 us
    pallas_call x1, Pallas kernels: 37.2 us -> 32.4 us  [fused_body(): pl.pallas_call(functools.partial(kernel, dp, space), out_shape=(jax.Shape...]
where the time goes in v3:
time: 36.8 us; the launch traced here: 36.6 us
  Pallas kernels  32.4 us (88%)
  local copies, waits for them, and re-layouts  3.62 us (10%)
  between operations  0.65 us (2%)
    pallas_call x1, Pallas kernels, fused_body(): pl.pallas_call(functools.partial(kernel, dp, space), out_shape=(jax.Shape...  32.4 us
    unnamed x4, local copies, waits for them, and re-layouts  3.62 us

profile of v3, /device:TPU:1, one launch (start us, length us, event | category | flops | bytes accessed | tf_op | source)
XLA Modules:
  0.0 36.6 jit_solution(11106133969572849447)
XLA Ops:
  0.6 32.4 %shard_map.86 = (bf16[1,24,32,1024]{3,2,1,0:T(8,128)(2,1)}, f32[16,72,128]{2,1,0:T(8,128)}) custom-call(bf16[1,24,32,1024]{3,2,1,0:T(8,128)(2,1)} %cot_hbm.1, f32[16,1,24,128]{3,2,1,0:T(8,128)} %spec_hbm.1, f32[16,24,24,128]{3,2,1,0:T(8,128)} %w_hbm.1, bf16[1024,256]{1,0:T(8,128)(2,1)} %constant.8.clone.into_hbm, ...), custom_call_target="tpu_custom_call" | custom-call | tf_op jit(solution)/shard_map/pallas_call | solution.py:538
  33.0 0.0 copy-start
  33.0 2.8 %copy.11 = bf16[1,24,32,1024]{3,2,1,0:T(8,128)(2,1)} copy(bf16[1,24,32,1024]{3,2,1,0:T(8,128)(2,1)} %get-tuple-element.4) | data formatting | bytes 3145728
  35.8 0.0 copy-done
  35.8 0.8 %copy.12 = f32[16,72,128]{2,1,0:T(8,128)} copy(f32[16,72,128]{2,1,0:T(8,128)S(1)} %copy-done) | data formatting | bytes 1179648
Async XLA Ops:
  33.0 2.8 %copy-start = (f32[16,72,128]{2,1,0:T(8,128)S(1)}, f32[16,72,128]{2,1,0:T(8,128)}, u32[]{:S(2)}) copy-start(f32[16,72,128]{2,1,0:T(8,128)} %get-tuple-element.5) | copy-start | bytes 1769476

commit v4 on v3

--- a/solution.py
+++ b/solution.py
@@ -135,9 +135,9 @@
 
 def kernel(
     dp, space,
-    cot_hbm, spec_hbm, w_hbm, into_hbm, rows_in_hbm, rows_out_hbm, out_of_hbm,
-    gin_hbm, gw_hbm,
-    gin_ref, gw_ref, cot, spec, w, into, rows_in, rows_out, out_of,
+    cot_hbm, spec_hbm, w_hbm, into_hbm, rows_in_hbm, rows_out_hbm,
+    back_hbm, gw_hbm,
+    back_ref, gw_ref, cot, spec, w, into, rows_in, rows_out,
     part, rs_in, gall, iall, back_sum, sp_out, sp_in, a_rows, b_rows,
     load_sem, store_sem, rs_send, rs_recv, ag_send, ag_recv, sp_send, sp_recv,
     up_send, down_send, sib_send, g_recv,
@@ -185,7 +185,6 @@
     l_spec = load(n + 1, spec_hbm.at[:, 0], spec)
     l_w = load(n + 2, w_hbm, w)
     l_rows_out = load(n + 3, rows_out_hbm.at[me_s], rows_out)
-    l_out_of = load(n + 4, out_of_hbm, out_of)
 
     lane = lax.broadcasted_iota(jnp.int32, (1, lanes), 1)
     lower = lane < half
@@ -359,11 +358,7 @@
             device_id_type=MESH,
         )
 
-    def sum_and_mix(h):
-        for t in range(1, space):
-            for piece in range(groups) if h == 0 else (groups,):
-                rs_copy(t, piece).wait_recv()
-
+    def summed(h):
         def gather_sum(k, carry):
             total = part[me_s * local + k]
             for t in range(1, space):
@@ -373,9 +368,8 @@
 
         lax.fori_loop(h * size, (h + 1) * size, gather_sum, 0, unroll=True)
         own_sends(h, lambda copy: copy.start())
-        if h == 0:
-            l_w.wait()
-
+
+    def mixed_by(h):
         def mix(k, carry):
             grad = gall[me_d, k]
             weight = w[k]
@@ -386,6 +380,8 @@
             return carry
 
         lax.fori_loop(h * size, (h + 1) * size, mix, 0, unroll=True)
+
+    def ag_start(h):
         for t in range(1, space):
             ag_copy(t, h).start()
 
@@ -441,11 +437,20 @@
             if h == 0:
                 back_sum[:, place] = found
             else:
-                columns_back(g, back_sum[:, place] + found)
-
-    def gin_store(g):
-        place = pl.ds(g * GROUP, GROUP)
-        return pltpu.make_async_copy(gin_ref.at[place], gin_hbm.at[0, place], store_sem.at[g])
+                found = back_sum[:, place] + found
+                high, low = split(
+                    jnp.concatenate(
+                        [found[:, i * lanes : (i + 1) * lanes] for i in range(GROUP)], axis=0
+                    )
+                )
+                place = pl.ds(g * GROUP * rows, GROUP * rows)
+                back_ref[place, pl.ds(0, lanes)] = high
+                back_ref[place, pl.ds(lanes, lanes)] = low
+                back_store(g).start()
+
+    def back_store(g):
+        place = pl.ds(g * GROUP * rows, GROUP * rows)
+        return pltpu.make_async_copy(back_ref.at[place], back_hbm.at[place], store_sem.at[g])
 
     def gw_store(h):
         place = pl.ds(h * size, size)
@@ -453,33 +458,28 @@
             gw_ref.at[place], gw_hbm.at[place], store_sem.at[groups + h]
         )
 
-    def columns_back(g, back):
-        back = jnp.concatenate(
-            [back[:, i * lanes : (i + 1) * lanes] for i in range(GROUP)], axis=0
-        )
-        high, low = split(back)
-        raster = jnp.dot(
-            jnp.concatenate([high, low, high], axis=1),
-            out_of[...],
-            preferred_element_type=jnp.float32,
-        )
-        gin_ref[pl.ds(g * GROUP, GROUP)] = raster.reshape(GROUP, rows, cols).astype(
-            jnp.bfloat16
-        )
-        gin_store(g).start()
-
-    sum_and_mix(0)
+    for t in range(1, space):
+        for piece in range(groups):
+            rs_copy(t, piece).wait_recv()
+    summed(0)
+    l_w.wait()
+    mixed_by(0)
     forward(1, 0)
     for t in range(1, dp):
         sp_arrival(t).wait_recv()
     for b in range(dp):
         rows_of(b)
-    sum_and_mix(1)
+    for t in range(1, space):
+        rs_copy(t, groups).wait_recv()
+    ag_start(0)
+    summed(1)
+    mixed_by(1)
+    ag_start(1)
     if nz > 2:
         forward(2, 0)
     pair_terms(me_d, 0)
+    pair_terms(me_d, 1)
     forward(1, 1)
-    pair_terms(me_d, 1)
     terms(1, 0)
     if nz > 3:
         forward(3, 0)
@@ -490,13 +490,13 @@
     terms(1, 1)
     if nz > 2:
         terms(2, 0)
-    l_out_of.wait()
+    if nz > 3:
+        terms(3, 0)
+        forward(3, 1)
     rows_back(1)
     if nz > 2:
         terms(2, 1)
     if nz > 3:
-        terms(3, 0)
-        forward(3, 1)
         terms(3, 1)
     for t in range(4, nz):
         for h in range(2):
@@ -520,9 +520,48 @@
         for t in range(1, nz):
             passed_on(t, h, leave, False)
     for g in range(groups):
-        gin_store(g).wait()
+        back_store(g).wait()
     for h in range(2):
         gw_store(h).wait()
+
+
+def columns_kernel(
+    back_hbm, terms_hbm, out_of_hbm, gin_hbm, gw_hbm,
+    back, terms, out_of, gin, load_sem, store_sem,
+):
+    channels, rows, cols = gin.shape
+    groups = channels // GROUP
+    lanes = back.shape[1] // 2
+    count = GROUP * rows
+    l_out_of = pltpu.make_async_copy(out_of_hbm, out_of, load_sem.at[groups])
+    l_out_of.start()
+    loads, stores = [], []
+    for g in range(groups):
+        place = pl.ds(g * count, count)
+        loads.append(pltpu.make_async_copy(back_hbm.at[place], back.at[place], load_sem.at[g]))
+        loads[g].start()
+    l_terms = pltpu.make_async_copy(terms_hbm, terms, load_sem.at[groups + 1])
+    l_terms.start()
+    l_out_of.wait()
+    for g in range(groups):
+        loads[g].wait()
+        both = back[pl.ds(g * count, count)]
+        raster = jnp.dot(
+            jnp.concatenate([both, both[:, :lanes]], axis=1),
+            out_of[...],
+            preferred_element_type=jnp.float32,
+        )
+        place = pl.ds(g * GROUP, GROUP)
+        gin[place] = raster.reshape(GROUP, rows, cols).astype(jnp.bfloat16)
+        stores.append(pltpu.make_async_copy(gin.at[place], gin_hbm.at[0, place], store_sem.at[g]))
+        stores[g].start()
+        if g == 0:
+            l_terms.wait()
+            s_terms = pltpu.make_async_copy(terms, gw_hbm, store_sem.at[groups])
+            s_terms.start()
+    for store in stores:
+        store.wait()
+    s_terms.wait()
 
 
 def fused_body(dp, space, cotangent, spectrum, weights):
@@ -535,16 +574,16 @@
     into, rows_in, rows_out, out_of = fixed
     f32 = jnp.float32
     dma = pltpu.SemaphoreType.DMA
-    return pl.pallas_call(
+    back, terms = pl.pallas_call(
         functools.partial(kernel, dp, space),
         out_shape=(
-            jax.ShapeDtypeStruct(cotangent.shape, jnp.bfloat16),
+            jax.ShapeDtypeStruct((channels * rows, 2 * lanes), jnp.bfloat16),
             jax.ShapeDtypeStruct((local, own * channels, lanes), f32),
         ),
-        in_specs=[pl.BlockSpec(memory_space=pl.ANY)] * 7,
+        in_specs=[pl.BlockSpec(memory_space=pl.ANY)] * 6,
         out_specs=[pl.BlockSpec(memory_space=pl.ANY)] * 2,
         scratch_shapes=[
-            pltpu.VMEM((channels, rows, cols), jnp.bfloat16),
+            pltpu.VMEM((channels * rows, 2 * lanes), jnp.bfloat16),
             pltpu.VMEM((local, own * channels, lanes), f32),
             pltpu.VMEM((channels, rows, cols), jnp.bfloat16),
             pltpu.VMEM((local, channels, lanes), f32),
@@ -552,7 +591,6 @@
             pltpu.VMEM(into.shape, jnp.bfloat16),
             pltpu.VMEM(rows_in.shape[1:], jnp.bfloat16),
             pltpu.VMEM(rows_out.shape[1:], jnp.bfloat16),
-            pltpu.VMEM(out_of.shape, jnp.bfloat16),
             pltpu.VMEM((modes, channels, lanes), f32),
             pltpu.VMEM((space - 1, local, channels, lanes), f32),
             pltpu.VMEM((dp, local, channels, lanes), f32),
@@ -562,7 +600,7 @@
             pltpu.VMEM((dp, local * own, lanes), f32),
             pltpu.VMEM((dp, local * own, lanes), f32),
             pltpu.VMEM((dp, local * own, lanes), f32),
-            dma((groups + 6,)),
+            dma((groups + 5,)),
             dma((groups + 2,)),
             dma((space - 1, groups + 1)),
             dma((space - 1, groups + 1)),
@@ -578,7 +616,25 @@
         compiler_params=pltpu.CompilerParams(
             collective_id=0, has_side_effects=True, vmem_limit_bytes=62 * 1024 * 1024
         ),
-    )(cotangent, spectrum, weights, into, rows_in, rows_out, out_of)
+    )(cotangent, spectrum, weights, into, rows_in, rows_out)
+    return pl.pallas_call(
+        columns_kernel,
+        out_shape=(
+            jax.ShapeDtypeStruct(cotangent.shape, jnp.bfloat16),
+            jax.ShapeDtypeStruct(terms.shape, f32),
+        ),
+        in_specs=[pl.BlockSpec(memory_space=pl.ANY)] * 3,
+        out_specs=[pl.BlockSpec(memory_space=pl.ANY)] * 2,
+        scratch_shapes=[
+            pltpu.VMEM(back.shape, jnp.bfloat16),
+            pltpu.VMEM(terms.shape, f32),
+            pltpu.VMEM(out_of.shape, jnp.bfloat16),
+            pltpu.VMEM(cotangent.shape[1:], jnp.bfloat16),
+            dma((groups + 2,)),
+            dma((groups + 1,)),
+        ],
+        compiler_params=pltpu.CompilerParams(vmem_limit_bytes=62 * 1024 * 1024),
+    )(back, terms, out_of)
 
 
 def solution(mesh):

time: 36.8 us -> 35.1 us (0.954)
  local copies, waits for them, and re-layouts: 3.62 us -> 0 us
  Pallas kernels: 32.4 us -> 34.3 us
    unnamed x4 -> x0, local copies, waits for them, and re-layouts: 3.62 us -> none
    pallas_call x0 -> x1, Pallas kernels: none -> 3.32 us  [fused_body(): pl.pallas_call(columns_kernel, out_shape=(jax.ShapeDtypeStruct(cotangent....]
    pallas_call x1, Pallas kernels: 32.4 us -> 31 us  [fused_body(): pl.pallas_call(functools.partial(kernel, dp, space), out_shape=(jax.Shape...]
where the time goes in v4:
time: 35.1 us; the launch traced here: 35 us
  Pallas kernels  34.3 us (98%)
  between operations  0.64 us (2%)
    pallas_call x1, Pallas kernels, fused_body(): pl.pallas_call(functools.partial(kernel, dp, space), out_shape=(jax.Shape...  31 us
    pallas_call x1, Pallas kernels, fused_body(): pl.pallas_call(columns_kernel, out_shape=(jax.ShapeDtypeStruct(cotangent....  3.32 us

profile of v4, /device:TPU:1, one launch (start us, length us, event | category | flops | bytes accessed | tf_op | source)
XLA Modules:
  0.0 35.0 jit_solution(8463498990452239404)
XLA Ops:
  0.6 31.0 %shard_map.86 = (bf16[768,256]{1,0:T(8,128)(2,1)}, f32[16,72,128]{2,1,0:T(8,128)}) custom-call(bf16[1,24,32,1024]{3,2,1,0:T(8,128)(2,1)} %cot_hbm.1, f32[16,1,24,128]{3,2,1,0:T(8,128)} %spec_hbm.1, f32[16,24,24,128]{3,2,1,0:T(8,128)} %w_hbm.1, bf16[1024,256]{1,0:T(8,128)(2,1)} %constant.8.clone.into_hbm, bf16[4,64,192]{2,1,0:T(8,128)(2,1)} %constant.9.clone.rows_in_hbm, ...), custom_call_target="tpu_custom_call" | custom-call | tf_op jit(solution)/shard_map/pallas_call | solution.py:577
  31.6 3.3 %shard_map.87 = (bf16[1,24,32,1024]{3,2,1,0:T(8,128)(2,1)}, f32[16,72,128]{2,1,0:T(8,128)}) custom-call(bf16[768,256]{1,0:T(8,128)(2,1)} %get-tuple-element.4.back_hbm, f32[16,72,128]{2,1,0:T(8,128)} %get-tuple-element.5.terms_hbm, bf16[384,1024]{1,0:T(8,128)(2,1)} %constant.11.clone.out_of_hbm), custom_call_target="tpu_custom_call" | custom-call | tf_op jit(solution)/shard_map/pallas_call | solution.py:620

commit v5 on v4

--- a/solution.py
+++ b/solution.py
@@ -12,6 +12,8 @@
 
 MESH = pl.DeviceIdType.MESH
 GROUP = 8
+COLUMNS = 4
+PARTS = 4
 
 
 def column_basis(col_count, modes_y):
@@ -119,8 +121,7 @@
     sines = np.sin(angle).reshape(modes, space, rows).transpose(1, 0, 2)
     high, low = halves(np.concatenate([cosines, sines], axis=2) / math.sqrt(height * cols))
     rows_in = np.concatenate([high, low, high], axis=2)
-    local = modes // space
-    order = np.arange(modes).reshape(space, 2, local // 2).transpose(1, 0, 2).reshape(2, -1)
+    order = np.arange(modes).reshape(space, PARTS, -1).transpose(1, 0, 2).reshape(PARTS, -1)
     both = np.concatenate([cosines[:, order], sines[:, order]], axis=2).transpose(0, 1, 3, 2)
     high, low = halves(both / math.sqrt(modes * modes_y))
     rows_out = np.concatenate([high, low, high], axis=3)
@@ -175,14 +176,14 @@
         copy.start()
         return copy
 
+    n = 1 + groups
+    l_spec = load(n + 1, spec_hbm.at[:, 0], spec)
     l_into = load(0, into_hbm, into)
     l_cot = []
     for g in range(groups):
         place = pl.ds(g * GROUP, GROUP)
         l_cot.append(load(1 + g, cot_hbm.at[0, place], cot.at[place]))
-    n = 1 + groups
     l_rows_in = load(n, rows_in_hbm.at[me_s], rows_in)
-    l_spec = load(n + 1, spec_hbm.at[:, 0], spec)
     l_w = load(n + 2, w_hbm, w)
     l_rows_out = load(n + 3, rows_out_hbm.at[me_s], rows_out)
 
@@ -193,14 +194,14 @@
     def turn(values):
         return pltpu.roll(values, half, values.ndim - 1)
 
-    size = local // 2
+    size = local // PARTS
 
     def rs_copy(t, piece):
         there = partner_s(t)
         if piece < groups:
             first, place = 0, pl.ds(piece * GROUP, GROUP)
         else:
-            first, place = size, pl.ds(0, channels)
+            first, place = (piece - groups + 1) * size, pl.ds(0, channels)
         return pltpu.make_async_remote_copy(
             part.at[pl.ds(there * local + first, size), place],
             rs_in.at[t - 1, pl.ds(first, size), place],
@@ -232,6 +233,14 @@
             device_id_type=MESH,
         )
 
+    l_spec.wait()
+    for d in range(dp):
+        for k in range(local):
+            sp_out[d, k * own : (k + 1) * own, :] = spec[k, d * own : (d + 1) * own, :]
+    pl.semaphore_wait(barrier, dp + space - 2)
+    for t in range(1, dp):
+        sp_copy(t).start()
+    sp_in[me_d] = sp_out[me_d]
     l_into.wait()
     l_rows_in.wait()
     for g in range(groups):
@@ -257,20 +266,12 @@
         )
         for i in range(GROUP):
             part[:, g * GROUP + i, :] = spectrum_part[:, i * lanes : (i + 1) * lanes]
-        if g == 0:
-            pl.semaphore_wait(barrier, dp + space - 2)
         for t in range(1, space):
             rs_copy(t, g).start()
-    for t in range(1, space):
-        rs_copy(t, groups).start()
-
-    l_spec.wait()
-    for d in range(dp):
-        for k in range(local):
-            sp_out[d, k * own : (k + 1) * own, :] = spec[k, d * own : (d + 1) * own, :]
-    for t in range(1, dp):
-        sp_copy(t).start()
-    sp_in[me_d] = sp_out[me_d]
+    for piece in range(groups, groups + PARTS - 1):
+        for t in range(1, space):
+            rs_copy(t, piece).start()
+
     gw_ref[...] = jnp.zeros_like(gw_ref)
 
     z, core = me_d // 2, lax.rem(me_d, 2)
@@ -436,6 +437,8 @@
             place = pl.ds(g * GROUP * lanes, GROUP * lanes)
             if h == 0:
                 back_sum[:, place] = found
+            elif h < PARTS - 1:
+                back_sum[:, place] += found
             else:
                 found = back_sum[:, place] + found
                 high, low = split(
@@ -452,77 +455,85 @@
         place = pl.ds(g * GROUP * rows, GROUP * rows)
         return pltpu.make_async_copy(back_ref.at[place], back_hbm.at[place], store_sem.at[g])
 
-    def gw_store(h):
-        place = pl.ds(h * size, size)
-        return pltpu.make_async_copy(
-            gw_ref.at[place], gw_hbm.at[place], store_sem.at[groups + h]
-        )
-
-    for t in range(1, space):
-        for piece in range(groups):
-            rs_copy(t, piece).wait_recv()
+    def gw_store():
+        return pltpu.make_async_copy(gw_ref, gw_hbm, store_sem.at[groups])
+
+    def arrived(h):
+        for t in range(1, space):
+            for piece in range(groups) if h == 0 else (groups + h - 1,):
+                rs_copy(t, piece).wait_recv()
+
+    def forward_some(*steps):
+        for t, h in steps:
+            if t < nz:
+                forward(t, h)
+
+    def terms_some(*steps):
+        for t, h in steps:
+            if t < nz:
+                terms(t, h)
+
+    arrived(0)
     summed(0)
     l_w.wait()
     mixed_by(0)
-    forward(1, 0)
+    arrived(1)
+    summed(1)
+    forward_some((1, 0))
+    mixed_by(1)
+    arrived(2)
+    summed(2)
+    forward_some((1, 1), (2, 0))
+    mixed_by(2)
     for t in range(1, dp):
         sp_arrival(t).wait_recv()
     for b in range(dp):
         rows_of(b)
-    for t in range(1, space):
-        rs_copy(t, groups).wait_recv()
-    ag_start(0)
-    summed(1)
-    mixed_by(1)
-    ag_start(1)
-    if nz > 2:
-        forward(2, 0)
-    pair_terms(me_d, 0)
-    pair_terms(me_d, 1)
-    forward(1, 1)
-    terms(1, 0)
-    if nz > 3:
-        forward(3, 0)
-    if nz > 2:
-        forward(2, 1)
+    arrived(3)
+    for h in range(3):
+        ag_start(h)
+    summed(3)
+    mixed_by(3)
+    ag_start(3)
+    forward_some((1, 2), (2, 1), (3, 0))
+    for h in range(PARTS):
+        pair_terms(me_d, h)
+    forward_some((1, 3), (2, 2), (3, 1))
+    terms_some((1, 0), (1, 1))
+    forward_some((2, 3), (3, 2))
     l_rows_out.wait()
     rows_back(0)
-    terms(1, 1)
-    if nz > 2:
-        terms(2, 0)
-    if nz > 3:
-        terms(3, 0)
-        forward(3, 1)
+    terms_some((1, 2), (1, 3), (2, 0))
     rows_back(1)
-    if nz > 2:
-        terms(2, 1)
-    if nz > 3:
-        terms(3, 1)
+    terms_some((2, 1), (3, 0), (2, 2))
+    forward_some((3, 3))
+    rows_back(2)
+    terms_some((3, 1), (2, 3), (3, 2))
+    rows_back(3)
+    terms_some((3, 3))
     for t in range(4, nz):
-        for h in range(2):
+        for h in range(PARTS):
             forward(t, h)
             terms(t, h)
-    for h in range(2):
-        gw_store(h).start()
+    gw_store().start()
 
     def leave(copy):
         copy.wait_send()
 
     for t in range(1, space):
-        for piece in range(groups + 1):
+        for piece in range(groups + PARTS - 1):
             rs_copy(t, piece).wait_send()
-        for h in range(2):
+        for h in range(PARTS):
             ag_copy(t, h).wait_send()
     for t in range(1, dp):
         sp_copy(t).wait_send()
-    for h in range(2):
+    for h in range(PARTS):
         own_sends(h, leave)
         for t in range(1, nz):
             passed_on(t, h, leave, False)
     for g in range(groups):
         back_store(g).wait()
-    for h in range(2):
-        gw_store(h).wait()
+    gw_store().wait()
 
 
 def columns_kernel(
@@ -530,9 +541,9 @@
     back, terms, out_of, gin, load_sem, store_sem,
 ):
     channels, rows, cols = gin.shape
-    groups = channels // GROUP
+    groups = channels // COLUMNS
     lanes = back.shape[1] // 2
-    count = GROUP * rows
+    count = COLUMNS * rows
     l_out_of = pltpu.make_async_copy(out_of_hbm, out_of, load_sem.at[groups])
     l_out_of.start()
     loads, stores = [], []
@@ -551,8 +562,8 @@
             out_of[...],
             preferred_element_type=jnp.float32,
         )
-        place = pl.ds(g * GROUP, GROUP)
-        gin[place] = raster.reshape(GROUP, rows, cols).astype(jnp.bfloat16)
+        place = pl.ds(g * COLUMNS, COLUMNS)
+        gin[place] = raster.reshape(COLUMNS, rows, cols).astype(jnp.bfloat16)
         stores.append(pltpu.make_async_copy(gin.at[place], gin_hbm.at[0, place], store_sem.at[g]))
         stores[g].start()
         if g == 0:
@@ -594,7 +605,7 @@
             pltpu.VMEM((modes, channels, lanes), f32),
             pltpu.VMEM((space - 1, local, channels, lanes), f32),
             pltpu.VMEM((dp, local, channels, lanes), f32),
-            pltpu.VMEM((2, modes // 2, channels, lanes), f32),
+            pltpu.VMEM((PARTS, modes // PARTS, channels, lanes), f32),
             pltpu.VMEM((rows, channels * lanes), f32),
             pltpu.VMEM((dp, local * own, lanes), f32),
             pltpu.VMEM((dp, local * own, lanes), f32),
@@ -602,16 +613,16 @@
             pltpu.VMEM((dp, local * own, lanes), f32),
             dma((groups + 5,)),
             dma((groups + 2,)),
-            dma((space - 1, groups + 1)),
-            dma((space - 1, groups + 1)),
-            dma((space - 1, 2)),
-            dma((space - 1, 2)),
+            dma((space - 1, groups + PARTS - 1)),
+            dma((space - 1, groups + PARTS - 1)),
+            dma((space - 1, PARTS)),
+            dma((space - 1, PARTS)),
             dma((dp,)),
             dma((dp,)),
-            dma((dp, 2)),
-            dma((dp, 2)),
-            dma((dp, 2)),
-            dma((dp, 2)),
+            dma((dp, PARTS)),
+            dma((dp, PARTS)),
+            dma((dp, PARTS)),
+            dma((dp, PARTS)),
         ],
         compiler_params=pltpu.CompilerParams(
             collective_id=0, has_side_effects=True, vmem_limit_bytes=62 * 1024 * 1024
@@ -630,8 +641,8 @@
             pltpu.VMEM(terms.shape, f32),
             pltpu.VMEM(out_of.shape, jnp.bfloat16),
             pltpu.VMEM(cotangent.shape[1:], jnp.bfloat16),
-            dma((groups + 2,)),
-            dma((groups + 1,)),
+            dma((channels // COLUMNS + 2,)),
+            dma((channels // COLUMNS + 1,)),
         ],
         compiler_params=pltpu.CompilerParams(vmem_limit_bytes=62 * 1024 * 1024),
     )(back, terms, out_of)
@@ -652,7 +663,7 @@
             and dp % 2 == 0
             and channels % dp == 0
             and channels % GROUP == 0
-            and spectrum.shape[0] % 2 == 0
+            and spectrum.shape[0] % PARTS == 0
             and rows % 16 == 0
             and (spectrum.shape[0] * (channels // dp)) % 8 == 0
         )

time: 35.1 us -> 36.2 us (1.031)
  Pallas kernels: 34.3 us -> 35.3 us
    pallas_call x1, Pallas kernels: 3.32 us -> 3.83 us  [fused_body(): pl.pallas_call(columns_kernel, out_shape=(jax.ShapeDtypeStruct(cotangent....]
    pallas_call x1, Pallas kernels: 31 us -> 31.4 us  [fused_body(): pl.pallas_call(functools.partial(kernel, dp, space), out_shape=(jax.Shape...]
where the time goes in v5:
time: 36.2 us; the launch traced here: 35.9 us
  Pallas kernels  35.3 us (98%)
  between operations  0.64 us (2%)
    pallas_call x1, Pallas kernels, fused_body(): pl.pallas_call(functools.partial(kernel, dp, space), out_shape=(jax.Shape...  31.4 us
    pallas_call x1, Pallas kernels, fused_body(): pl.pallas_call(columns_kernel, out_shape=(jax.ShapeDtypeStruct(cotangent....  3.83 us

profile of v5, /device:TPU:1, one launch (start us, length us, event | category | flops | bytes accessed | tf_op | source)
XLA Modules:
  0.0 35.9 jit_solution(3718087007374399501)
XLA Ops:
  0.6 31.4 %shard_map.86 = (bf16[768,256]{1,0:T(8,128)(2,1)}, f32[16,72,128]{2,1,0:T(8,128)}) custom-call(bf16[1,24,32,1024]{3,2,1,0:T(8,128)(2,1)} %cot_hbm.1, f32[16,1,24,128]{3,2,1,0:T(8,128)} %spec_hbm.1, f32[16,24,24,128]{3,2,1,0:T(8,128)} %w_hbm.1, bf16[1024,256]{1,0:T(8,128)(2,1)} %constant.8.clone.into_hbm, bf16[4,64,192]{2,1,0:T(8,128)(2,1)} %constant.9.clone.rows_in_hbm, ...), custom_call_target="tpu_custom_call" | custom-call | tf_op jit(solution)/shard_map/pallas_call | solution.py:588
  32.1 3.8 %shard_map.87 = (bf16[1,24,32,1024]{3,2,1,0:T(8,128)(2,1)}, f32[16,72,128]{2,1,0:T(8,128)}) custom-call(bf16[768,256]{1,0:T(8,128)(2,1)} %get-tuple-element.4.back_hbm, f32[16,72,128]{2,1,0:T(8,128)} %get-tuple-element.5.terms_hbm, bf16[384,1024]{1,0:T(8,128)(2,1)} %constant.11.clone.out_of_hbm), custom_call_target="tpu_custom_call" | custom-call | tf_op jit(solution)/shard_map/pallas_call | solution.py:631

commit v6 on v4

--- a/solution.py
+++ b/solution.py
@@ -12,6 +12,7 @@
 
 MESH = pl.DeviceIdType.MESH
 GROUP = 8
+COLUMNS = 256
 
 
 def column_basis(col_count, modes_y):
@@ -108,6 +109,12 @@
     return high, low
 
 
+def stack(high, low):
+    above = np.concatenate([high, high], axis=-1)
+    below = np.concatenate([low, np.zeros_like(low)], axis=-1)
+    return np.concatenate([above, below], axis=-2)
+
+
 def tables(modes, modes_y, rows, cols, space):
     height = rows * space
     angle = 2.0 * np.pi * (np.outer(np.arange(cols), np.arange(modes_y)) % cols) / cols
@@ -118,12 +125,12 @@
     cosines = np.cos(angle).reshape(modes, space, rows).transpose(1, 0, 2)
     sines = np.sin(angle).reshape(modes, space, rows).transpose(1, 0, 2)
     high, low = halves(np.concatenate([cosines, sines], axis=2) / math.sqrt(height * cols))
-    rows_in = np.concatenate([high, low, high], axis=2)
+    rows_in = stack(high, low)
     local = modes // space
     order = np.arange(modes).reshape(space, 2, local // 2).transpose(1, 0, 2).reshape(2, -1)
     both = np.concatenate([cosines[:, order], sines[:, order]], axis=2).transpose(0, 1, 3, 2)
     high, low = halves(both / math.sqrt(modes * modes_y))
-    rows_out = np.concatenate([high, low, high], axis=3)
+    rows_out = stack(high, low)
     return into, rows_in, rows_out, out_of
 
 
@@ -232,6 +239,15 @@
             device_id_type=MESH,
         )
 
+    def send_spectrum():
+        l_spec.wait()
+        for d in range(dp):
+            for k in range(local):
+                sp_out[d, k * own : (k + 1) * own, :] = spec[k, d * own : (d + 1) * own, :]
+        for t in range(1, dp):
+            sp_copy(t).start()
+        sp_in[me_d] = sp_out[me_d]
+
     l_into.wait()
     l_rows_in.wait()
     for g in range(groups):
@@ -252,25 +268,21 @@
         high, low = split(stacked)
         spectrum_part = jnp.dot(
             rows_in[...],
-            jnp.concatenate([high, high, low], axis=0),
+            jnp.concatenate([high, low], axis=0),
             preferred_element_type=jnp.float32,
         )
+        spectrum_part = spectrum_part[:modes] + spectrum_part[modes:]
         for i in range(GROUP):
             part[:, g * GROUP + i, :] = spectrum_part[:, i * lanes : (i + 1) * lanes]
         if g == 0:
             pl.semaphore_wait(barrier, dp + space - 2)
         for t in range(1, space):
             rs_copy(t, g).start()
+        if g == 0:
+            send_spectrum()
     for t in range(1, space):
         rs_copy(t, groups).start()
 
-    l_spec.wait()
-    for d in range(dp):
-        for k in range(local):
-            sp_out[d, k * own : (k + 1) * own, :] = spec[k, d * own : (d + 1) * own, :]
-    for t in range(1, dp):
-        sp_copy(t).start()
-    sp_in[me_d] = sp_out[me_d]
     gw_ref[...] = jnp.zeros_like(gw_ref)
 
     z, core = me_d // 2, lax.rem(me_d, 2)
@@ -430,9 +442,10 @@
             high, low = split(jnp.concatenate([mixed, turned], axis=0))
             found = jnp.dot(
                 rows_out[h],
-                jnp.concatenate([high, high, low], axis=0),
+                jnp.concatenate([high, low], axis=0),
                 preferred_element_type=jnp.float32,
             )
+            found = found[:rows] + found[rows:]
             place = pl.ds(g * GROUP * lanes, GROUP * lanes)
             if h == 0:
                 back_sum[:, place] = found
@@ -530,34 +543,34 @@
     back, terms, out_of, gin, load_sem, store_sem,
 ):
     channels, rows, cols = gin.shape
-    groups = channels // GROUP
     lanes = back.shape[1] // 2
-    count = GROUP * rows
-    l_out_of = pltpu.make_async_copy(out_of_hbm, out_of, load_sem.at[groups])
-    l_out_of.start()
+    pieces = cols // COLUMNS
+    l_back = pltpu.make_async_copy(back_hbm, back, load_sem.at[pieces])
+    l_back.start()
     loads, stores = [], []
-    for g in range(groups):
-        place = pl.ds(g * count, count)
-        loads.append(pltpu.make_async_copy(back_hbm.at[place], back.at[place], load_sem.at[g]))
+    for g in range(pieces):
+        place = pl.ds(g * COLUMNS, COLUMNS)
+        loads.append(
+            pltpu.make_async_copy(out_of_hbm.at[:, place], out_of.at[:, place], load_sem.at[g])
+        )
         loads[g].start()
-    l_terms = pltpu.make_async_copy(terms_hbm, terms, load_sem.at[groups + 1])
+    l_terms = pltpu.make_async_copy(terms_hbm, terms, load_sem.at[pieces + 1])
     l_terms.start()
-    l_out_of.wait()
-    for g in range(groups):
+    l_back.wait()
+    both = back[...]
+    both = jnp.concatenate([both, both[:, :lanes]], axis=1)
+    for g in range(pieces):
         loads[g].wait()
-        both = back[pl.ds(g * count, count)]
-        raster = jnp.dot(
-            jnp.concatenate([both, both[:, :lanes]], axis=1),
-            out_of[...],
-            preferred_element_type=jnp.float32,
-        )
-        place = pl.ds(g * GROUP, GROUP)
-        gin[place] = raster.reshape(GROUP, rows, cols).astype(jnp.bfloat16)
-        stores.append(pltpu.make_async_copy(gin.at[place], gin_hbm.at[0, place], store_sem.at[g]))
+        place = pl.ds(g * COLUMNS, COLUMNS)
+        raster = jnp.dot(both, out_of[:, place], preferred_element_type=jnp.float32)
+        gin[:, :, place] = raster.reshape(channels, rows, COLUMNS).astype(jnp.bfloat16)
+        stores.append(
+            pltpu.make_async_copy(gin.at[:, :, place], gin_hbm.at[0, :, :, place], store_sem.at[g])
+        )
         stores[g].start()
         if g == 0:
             l_terms.wait()
-            s_terms = pltpu.make_async_copy(terms, gw_hbm, store_sem.at[groups])
+            s_terms = pltpu.make_async_copy(terms, gw_hbm, store_sem.at[pieces])
             s_terms.start()
     for store in stores:
         store.wait()
@@ -630,8 +643,8 @@
             pltpu.VMEM(terms.shape, f32),
             pltpu.VMEM(out_of.shape, jnp.bfloat16),
             pltpu.VMEM(cotangent.shape[1:], jnp.bfloat16),
-            dma((groups + 2,)),
-            dma((groups + 1,)),
+            dma((cols // COLUMNS + 2,)),
+            dma((cols // COLUMNS + 1,)),
         ],
         compiler_params=pltpu.CompilerParams(vmem_limit_bytes=62 * 1024 * 1024),
     )(back, terms, out_of)
@@ -652,6 +665,7 @@
             and dp % 2 == 0
             and channels % dp == 0
             and channels % GROUP == 0
+            and cotangent.shape[3] % COLUMNS == 0
             and spectrum.shape[0] % 2 == 0
             and rows % 16 == 0
             and (spectrum.shape[0] * (channels // dp)) % 8 == 0

time: 35.1 us -> 35.9 us (1.023)
  Pallas kernels: 34.3 us -> 35.1 us
    pallas_call x1, Pallas kernels: 3.32 us -> 4.12 us  [fused_body(): pl.pallas_call(columns_kernel, out_shape=(jax.ShapeDtypeStruct(cotangent....]
where the time goes in v6:
time: 35.9 us; the launch traced here: 35.8 us
  Pallas kernels  35.1 us (98%)
  between operations  0.64 us (2%)
    pallas_call x1, Pallas kernels, fused_body(): pl.pallas_call(functools.partial(kernel, dp, space), out_shape=(jax.Shape...  31 us
    pallas_call x1, Pallas kernels, fused_body(): pl.pallas_call(columns_kernel, out_shape=(jax.ShapeDtypeStruct(cotangent....  4.12 us

profile of v6, /device:TPU:1, one launch (start us, length us, event | category | flops | bytes accessed | tf_op | source)
XLA Modules:
  0.0 35.8 jit_solution(14214355190456602115)
XLA Ops:
  0.6 31.0 %shard_map.86 = (bf16[768,256]{1,0:T(8,128)(2,1)}, f32[16,72,128]{2,1,0:T(8,128)}) custom-call(bf16[1,24,32,1024]{3,2,1,0:T(8,128)(2,1)} %cot_hbm.1, f32[16,1,24,128]{3,2,1,0:T(8,128)} %spec_hbm.1, f32[16,24,24,128]{3,2,1,0:T(8,128)} %w_hbm.1, bf16[1024,256]{1,0:T(8,128)(2,1)} %constant.8.clone.into_hbm, bf16[4,128,128]{2,1,0:T(8,128)(2,1)} %constant.9.clone.rows_in_hbm, ...), custom_call_target="tpu_custom_call" | custom-call | tf_op jit(solution)/shard_map/pallas_call | solution.py:590
  31.6 4.1 %shard_map.87 = (bf16[1,24,32,1024]{3,2,1,0:T(8,128)(2,1)}, f32[16,72,128]{2,1,0:T(8,128)}) custom-call(bf16[768,256]{1,0:T(8,128)(2,1)} %get-tuple-element.4.back_hbm, f32[16,72,128]{2,1,0:T(8,128)} %get-tuple-element.5.terms_hbm, bf16[384,1024]{1,0:T(8,128)(2,1)} %constant.11.clone.out_of_hbm), custom_call_target="tpu_custom_call" | custom-call | tf_op jit(solution)/shard_map/pallas_call | solution.py:633

commit v7 on v4

--- a/solution.py
+++ b/solution.py
@@ -108,6 +108,12 @@
     return high, low
 
 
+def stack(high, low):
+    above = np.concatenate([high, high], axis=-1)
+    below = np.concatenate([low, np.zeros_like(low)], axis=-1)
+    return np.concatenate([above, below], axis=-2)
+
+
 def tables(modes, modes_y, rows, cols, space):
     height = rows * space
     angle = 2.0 * np.pi * (np.outer(np.arange(cols), np.arange(modes_y)) % cols) / cols
@@ -118,12 +124,12 @@
     cosines = np.cos(angle).reshape(modes, space, rows).transpose(1, 0, 2)
     sines = np.sin(angle).reshape(modes, space, rows).transpose(1, 0, 2)
     high, low = halves(np.concatenate([cosines, sines], axis=2) / math.sqrt(height * cols))
-    rows_in = np.concatenate([high, low, high], axis=2)
+    rows_in = stack(high, low)
     local = modes // space
     order = np.arange(modes).reshape(space, 2, local // 2).transpose(1, 0, 2).reshape(2, -1)
     both = np.concatenate([cosines[:, order], sines[:, order]], axis=2).transpose(0, 1, 3, 2)
     high, low = halves(both / math.sqrt(modes * modes_y))
-    rows_out = np.concatenate([high, low, high], axis=3)
+    rows_out = stack(high, low)
     return into, rows_in, rows_out, out_of
 
 
@@ -232,6 +238,15 @@
             device_id_type=MESH,
         )
 
+    def send_spectrum():
+        l_spec.wait()
+        for d in range(dp):
+            for k in range(local):
+                sp_out[d, k * own : (k + 1) * own, :] = spec[k, d * own : (d + 1) * own, :]
+        for t in range(1, dp):
+            sp_copy(t).start()
+        sp_in[me_d] = sp_out[me_d]
+
     l_into.wait()
     l_rows_in.wait()
     for g in range(groups):
@@ -252,25 +267,21 @@
         high, low = split(stacked)
         spectrum_part = jnp.dot(
             rows_in[...],
-            jnp.concatenate([high, high, low], axis=0),
+            jnp.concatenate([high, low], axis=0),
             preferred_element_type=jnp.float32,
         )
+        spectrum_part = spectrum_part[:modes] + spectrum_part[modes:]
         for i in range(GROUP):
             part[:, g * GROUP + i, :] = spectrum_part[:, i * lanes : (i + 1) * lanes]
         if g == 0:
             pl.semaphore_wait(barrier, dp + space - 2)
         for t in range(1, space):
             rs_copy(t, g).start()
+        if g == 0:
+            send_spectrum()
     for t in range(1, space):
         rs_copy(t, groups).start()
 
-    l_spec.wait()
-    for d in range(dp):
-        for k in range(local):
-            sp_out[d, k * own : (k + 1) * own, :] = spec[k, d * own : (d + 1) * own, :]
-    for t in range(1, dp):
-        sp_copy(t).start()
-    sp_in[me_d] = sp_out[me_d]
     gw_ref[...] = jnp.zeros_like(gw_ref)
 
     z, core = me_d // 2, lax.rem(me_d, 2)
@@ -430,9 +441,10 @@
             high, low = split(jnp.concatenate([mixed, turned], axis=0))
             found = jnp.dot(
                 rows_out[h],
-                jnp.concatenate([high, high, low], axis=0),
+                jnp.concatenate([high, low], axis=0),
                 preferred_element_type=jnp.float32,
             )
+            found = found[:rows] + found[rows:]
             place = pl.ds(g * GROUP * lanes, GROUP * lanes)
             if h == 0:
                 back_sum[:, place] = found
@@ -464,6 +476,7 @@
     summed(0)
     l_w.wait()
     mixed_by(0)
+    ag_start(0)
     forward(1, 0)
     for t in range(1, dp):
         sp_arrival(t).wait_recv()
@@ -471,7 +484,6 @@
         rows_of(b)
     for t in range(1, space):
         rs_copy(t, groups).wait_recv()
-    ag_start(0)
     summed(1)
     mixed_by(1)
     ag_start(1)

time: 35.1 us -> 35.2 us (level)
  no operation moved by 1% of the time
where the time goes in v7:
time: 35.2 us; the launch traced here: 35.1 us
  Pallas kernels  34.4 us (98%)
  between operations  0.64 us (2%)
    pallas_call x1, Pallas kernels, fused_body(): pl.pallas_call(functools.partial(kernel, dp, space), out_shape=(jax.Shape...  31.1 us
    pallas_call x1, Pallas kernels, fused_body(): pl.pallas_call(columns_kernel, out_shape=(jax.ShapeDtypeStruct(cotangent....  3.33 us

profile of v7, /device:TPU:1, one launch (start us, length us, event | category | flops | bytes accessed | tf_op | source)
XLA Modules:
  0.0 35.1 jit_solution(474969380650959450)
XLA Ops:
  0.6 31.1 %shard_map.86 = (bf16[768,256]{1,0:T(8,128)(2,1)}, f32[16,72,128]{2,1,0:T(8,128)}) custom-call(bf16[1,24,32,1024]{3,2,1,0:T(8,128)(2,1)} %cot_hbm.1, f32[16,1,24,128]{3,2,1,0:T(8,128)} %spec_hbm.1, f32[16,24,24,128]{3,2,1,0:T(8,128)} %w_hbm.1, bf16[1024,256]{1,0:T(8,128)(2,1)} %constant.8.clone.into_hbm, bf16[4,128,128]{2,1,0:T(8,128)(2,1)} %constant.9.clone.rows_in_hbm, ...), custom_call_target="tpu_custom_call" | custom-call | tf_op jit(solution)/shard_map/pallas_call | solution.py:589
  31.8 3.3 %shard_map.87 = (bf16[1,24,32,1024]{3,2,1,0:T(8,128)(2,1)}, f32[16,72,128]{2,1,0:T(8,128)}) custom-call(bf16[768,256]{1,0:T(8,128)(2,1)} %get-tuple-element.4.back_hbm, f32[16,72,128]{2,1,0:T(8,128)} %get-tuple-element.5.terms_hbm, bf16[384,1024]{1,0:T(8,128)(2,1)} %constant.11.clone.out_of_hbm), custom_call_target="tpu_custom_call" | custom-call | tf_op jit(solution)/shard_map/pallas_call | solution.py:632

commit v8 on v7

--- a/solution.py
+++ b/solution.py
@@ -141,9 +141,9 @@
 
 def kernel(
     dp, space,
-    cot_hbm, spec_hbm, w_hbm, into_hbm, rows_in_hbm, rows_out_hbm,
+    cot_hbm, spec_hbm, w_hbm, into_hbm, rows_in_hbm, rows_out_hbm, out_of_hbm,
     back_hbm, gw_hbm,
-    back_ref, gw_ref, cot, spec, w, into, rows_in, rows_out,
+    back_ref, gw_ref, cot, spec, w, into, rows_in, rows_out, out_of,
     part, rs_in, gall, iall, back_sum, sp_out, sp_in, a_rows, b_rows,
     load_sem, store_sem, rs_send, rs_recv, ag_send, ag_recv, sp_send, sp_recv,
     up_send, down_send, sib_send, g_recv,
@@ -191,6 +191,7 @@
     l_spec = load(n + 1, spec_hbm.at[:, 0], spec)
     l_w = load(n + 2, w_hbm, w)
     l_rows_out = load(n + 3, rows_out_hbm.at[me_s], rows_out)
+    l_out_of = load(n + 4, out_of_hbm, out_of)
 
     lane = lax.broadcasted_iota(jnp.int32, (1, lanes), 1)
     lower = lane < half
@@ -455,14 +456,19 @@
                         [found[:, i * lanes : (i + 1) * lanes] for i in range(GROUP)], axis=0
                     )
                 )
-                place = pl.ds(g * GROUP * rows, GROUP * rows)
-                back_ref[place, pl.ds(0, lanes)] = high
-                back_ref[place, pl.ds(lanes, lanes)] = low
+                raster = jnp.dot(
+                    jnp.concatenate([high, low, high], axis=1),
+                    out_of[...],
+                    preferred_element_type=jnp.float32,
+                )
+                back_ref[pl.ds(g * GROUP, GROUP)] = raster.reshape(GROUP, rows, cols).astype(
+                    jnp.bfloat16
+                )
                 back_store(g).start()
 
     def back_store(g):
-        place = pl.ds(g * GROUP * rows, GROUP * rows)
-        return pltpu.make_async_copy(back_ref.at[place], back_hbm.at[place], store_sem.at[g])
+        place = pl.ds(g * GROUP, GROUP)
+        return pltpu.make_async_copy(back_ref.at[place], back_hbm.at[0, place], store_sem.at[g])
 
     def gw_store(h):
         place = pl.ds(h * size, size)
@@ -505,6 +511,7 @@
     if nz > 3:
         terms(3, 0)
         forward(3, 1)
+    l_out_of.wait()
     rows_back(1)
     if nz > 2:
         terms(2, 1)
@@ -537,43 +544,18 @@
         gw_store(h).wait()
 
 
-def columns_kernel(
-    back_hbm, terms_hbm, out_of_hbm, gin_hbm, gw_hbm,
-    back, terms, out_of, gin, load_sem, store_sem,
-):
-    channels, rows, cols = gin.shape
-    groups = channels // GROUP
-    lanes = back.shape[1] // 2
-    count = GROUP * rows
-    l_out_of = pltpu.make_async_copy(out_of_hbm, out_of, load_sem.at[groups])
-    l_out_of.start()
-    loads, stores = [], []
-    for g in range(groups):
-        place = pl.ds(g * count, count)
-        loads.append(pltpu.make_async_copy(back_hbm.at[place], back.at[place], load_sem.at[g]))
-        loads[g].start()
-    l_terms = pltpu.make_async_copy(terms_hbm, terms, load_sem.at[groups + 1])
-    l_terms.start()
-    l_out_of.wait()
-    for g in range(groups):
-        loads[g].wait()
-        both = back[pl.ds(g * count, count)]
-        raster = jnp.dot(
-            jnp.concatenate([both, both[:, :lanes]], axis=1),
-            out_of[...],
-            preferred_element_type=jnp.float32,
-        )
+def store_kernel(gin_hbm, terms_hbm, gin_out, gw_out, sem):
+    copies = [pltpu.make_async_copy(terms_hbm, gw_out, sem.at[0])]
+    channels = gin_hbm.shape[1]
+    for g in range(channels // GROUP):
         place = pl.ds(g * GROUP, GROUP)
-        gin[place] = raster.reshape(GROUP, rows, cols).astype(jnp.bfloat16)
-        stores.append(pltpu.make_async_copy(gin.at[place], gin_hbm.at[0, place], store_sem.at[g]))
-        stores[g].start()
-        if g == 0:
-            l_terms.wait()
-            s_terms = pltpu.make_async_copy(terms, gw_hbm, store_sem.at[groups])
-            s_terms.start()
-    for store in stores:
-        store.wait()
-    s_terms.wait()
+        copies.append(
+            pltpu.make_async_copy(gin_hbm.at[0, place], gin_out.at[0, place], sem.at[1 + g])
+        )
+    for copy in copies:
+        copy.start()
+    for copy in copies:
+        copy.wait()
 
 
 def fused_body(dp, space, cotangent, spectrum, weights):
@@ -589,13 +571,13 @@
     back, terms = pl.pallas_call(
         functools.partial(kernel, dp, space),
         out_shape=(
-            jax.ShapeDtypeStruct((channels * rows, 2 * lanes), jnp.bfloat16),
+            jax.ShapeDtypeStruct(cotangent.shape, jnp.bfloat16),
             jax.ShapeDtypeStruct((local, own * channels, lanes), f32),
         ),
-        in_specs=[pl.BlockSpec(memory_space=pl.ANY)] * 6,
+        in_specs=[pl.BlockSpec(memory_space=pl.ANY)] * 7,
         out_specs=[pl.BlockSpec(memory_space=pl.ANY)] * 2,
         scratch_shapes=[
-            pltpu.VMEM((channels * rows, 2 * lanes), jnp.bfloat16),
+            pltpu.VMEM((channels, rows, cols), jnp.bfloat16),
             pltpu.VMEM((local, own * channels, lanes), f32),
             pltpu.VMEM((channels, rows, cols), jnp.bfloat16),
             pltpu.VMEM((local, channels, lanes), f32),
@@ -603,6 +585,7 @@
             pltpu.VMEM(into.shape, jnp.bfloat16),
             pltpu.VMEM(rows_in.shape[1:], jnp.bfloat16),
             pltpu.VMEM(rows_out.shape[1:], jnp.bfloat16),
+            pltpu.VMEM(out_of.shape, jnp.bfloat16),
             pltpu.VMEM((modes, channels, lanes), f32),
             pltpu.VMEM((space - 1, local, channels, lanes), f32),
             pltpu.VMEM((dp, local, channels, lanes), f32),
@@ -612,7 +595,7 @@
             pltpu.VMEM((dp, local * own, lanes), f32),
             pltpu.VMEM((dp, local * own, lanes), f32),
             pltpu.VMEM((dp, local * own, lanes), f32),
-            dma((groups + 5,)),
+            dma((groups + 6,)),
             dma((groups + 2,)),
             dma((space - 1, groups + 1)),
             dma((space - 1, groups + 1)),
@@ -628,25 +611,18 @@
         compiler_params=pltpu.CompilerParams(
             collective_id=0, has_side_effects=True, vmem_limit_bytes=62 * 1024 * 1024
         ),
-    )(cotangent, spectrum, weights, into, rows_in, rows_out)
+    )(cotangent, spectrum, weights, into, rows_in, rows_out, out_of)
     return pl.pallas_call(
-        columns_kernel,
+        store_kernel,
         out_shape=(
             jax.ShapeDtypeStruct(cotangent.shape, jnp.bfloat16),
             jax.ShapeDtypeStruct(terms.shape, f32),
         ),
-        in_specs=[pl.BlockSpec(memory_space=pl.ANY)] * 3,
+        in_specs=[pl.BlockSpec(memory_space=pl.ANY)] * 2,
         out_specs=[pl.BlockSpec(memory_space=pl.ANY)] * 2,
-        scratch_shapes=[
-            pltpu.VMEM(back.shape, jnp.bfloat16),
-            pltpu.VMEM(terms.shape, f32),
-            pltpu.VMEM(out_of.shape, jnp.bfloat16),
-            pltpu.VMEM(cotangent.shape[1:], jnp.bfloat16),
-            dma((groups + 2,)),
-            dma((groups + 1,)),
-        ],
+        scratch_shapes=[dma((groups + 1,))],
         compiler_params=pltpu.CompilerParams(vmem_limit_bytes=62 * 1024 * 1024),
-    )(back, terms, out_of)
+    )(back, terms)
 
 
 def solution(mesh):

time: 35.2 us -> 99.6 us (2.83)
  Pallas kernels: 34.4 us -> 97.9 us
    pallas_call x1, Pallas kernels: 3.33 us -> 66.7 us  [fused_body(): pl.pallas_call(store_kernel, out_shape=(jax.ShapeDtypeStruct(cotangent.sh...]
where the time goes in v8:
time: 99.6 us; the launch traced here: 98.5 us
  Pallas kernels  97.9 us (98%)
    pallas_call x1, Pallas kernels, fused_body(): pl.pallas_call(store_kernel, out_shape=(jax.ShapeDtypeStruct(cotangent.sh...  66.7 us
    pallas_call x1, Pallas kernels, fused_body(): pl.pallas_call(functools.partial(kernel, dp, space), out_shape=(jax.Shape...  31.2 us

profile of v8, /device:TPU:1, one launch (start us, length us, event | category | flops | bytes accessed | tf_op | source)
XLA Modules:
  0.0 98.5 jit_solution(5012910931316868656)
XLA Ops:
  0.6 31.2 %shard_map.86 = (bf16[1,24,32,1024]{3,2,1,0:T(8,128)(2,1)}, f32[16,72,128]{2,1,0:T(8,128)}) custom-call(bf16[1,24,32,1024]{3,2,1,0:T(8,128)(2,1)} %cot_hbm.1, f32[16,1,24,128]{3,2,1,0:T(8,128)} %spec_hbm.1, f32[16,24,24,128]{3,2,1,0:T(8,128)} %w_hbm.1, bf16[1024,256]{1,0:T(8,128)(2,1)} %constant.8.clone.into_hbm, ...), custom_call_target="tpu_custom_call" | custom-call | tf_op jit(solution)/shard_map/pallas_call | solution.py:571
  31.9 66.7 %shard_map.87 = (bf16[1,24,32,1024]{3,2,1,0:T(8,128)(2,1)}, f32[16,72,128]{2,1,0:T(8,128)}) custom-call(bf16[1,24,32,1024]{3,2,1,0:T(8,128)(2,1)} %get-tuple-element.4.gin_hbm, f32[16,72,128]{2,1,0:T(8,128)} %get-tuple-element.5.terms_hbm), custom_call_target="tpu_custom_call" | custom-call | tf_op jit(solution)/shard_map/pallas_call | solution.py:615
